TPU v7x, 32 devices: a whole 2x2x4 slice. The times are simulated.
32 devices in a mesh: col: 16 (over z, y, x), row: 2 (over core).
Axes of the slice: x: 2, y: 2, z: 4, core: 2. Of those that a mesh axis runs over, the one named last changes fastest.
Arguments:
- static_flex: float32 [2048, 8192], P('row', 'col'), may hold values from -6 to 6
- phi_slab: float32 [2048, 1024], P('row', 'col'), may hold values from -6 to 6
- phi_cols: float32 [8192, 1024], P('col', 'row'), may hold values from -6 to 6
- eigenvalues: float32 [1024], P('col'), may hold values from 8 to 128
Outputs:
- residual_flex: float32 [2048, 8192], P('row', 'col')
All inputs are finite; a program needn't handle non-finite values.
Results may differ from a plain program's by a relative error of at most 0.00005.
Values sent between devices are 32-bit elements; how exact they have to be, the bound alone decides.
No kernel may reach another device: no remote copies, remote signals or barrier semaphores. Data moves between devices by JAX's collectives and lax.ppermute only.
A program may use at most 64 MiB of HBM per device.

v0:
```python
import jax
import jax.numpy as jnp
from jax import lax
from jax.sharding import PartitionSpec as P


def outer_modes(left, right):
    return lax.dot_general(
        left,
        right,
        (((1,), (1,)), ((), ())),
        precision=lax.Precision.HIGHEST,
        preferred_element_type=jnp.float32,
    )


def local(static_flex, phi_slab, phi_cols, eigenvalues):
    scaled = phi_slab / eigenvalues[None, :]
    rows_all = lax.all_gather(scaled, "col", axis=1, tiled=True)
    cols_all = lax.all_gather(phi_cols, "row", axis=1, tiled=True)
    result = static_flex - outer_modes(rows_all, cols_all)
    return result


def solution(mesh):
    placed = (P("row", "col"), P("row", "col"), P("col", "row"), P("col"))
    return jax.shard_map(
        local, mesh=mesh, in_specs=placed, out_specs=P("row", "col"), check_vma=False
    )
```

profile of v0, /device:TPU:0, one launch (start us, length us, event | category | flops | bytes accessed | tf_op | source)
XLA Modules:
  0.0 126.1 jit_solution(12578865902759359108)
XLA Ops:
  6.5 0.0 all-gather.5.cloned.1.call-start
  6.5 0.7 all-gather.5.cloned.1.call-update
  7.3 0.0 all-gather.3.cloned.1.call-start
  7.3 1.7 %broadcast_divide_fusion = f32[1024,64]{0,1:T(8,128)} fusion(f32[1024,64]{0,1:T(8,128)} %param.5, f32[64]{0:T(128)} %param.7), kind=kLoop, calls=%fused_computation.1 | loop fusion | flops 65536 | bytes 524544 | tf_op jit(solution)/shard_map/div | solution.py:18
  9.0 0.0 all-gather.3.cloned.1.call-update
  9.1 13.1 %all-gather.5.cloned.1.call-done = f32[512,1024]{1,0:T(8,128)} async-done(((f32[512,512]{1,0:T(8,128)}), f32[512,1024]{1,0:T(8,128)}) %all-gather.5.cloned.1.call-update) | async-done | bytes 2097168 | tf_op jit(solution)/shard_map/all_gather | solution.py:20
  22.2 80.1 %all-gather.3.cloned.1.call-done = f32[1024,1024]{0,1:T(8,128)} async-done(((f32[1024,64]{0,1:T(8,128)}), f32[1024,1024]{0,1:T(8,128)}) %all-gather.3.cloned.1.call-update) | async-done | bytes 4194320 | tf_op jit(solution)/shard_map/all_gather | solution.py:19
  102.3 16.9 %convolution_subtract_fusion = f32[1024,512]{1,0:T(8,128)} fusion(f32[1024,512]{1,0:T(8,128)} %param.4, f32[1024,1024]{0,1:T(8,128)} %all-gather.3.cloned.1.call-done, f32[512,1024]{1,0:T(8,128)} %all-gather.5.cloned.1.call-done), kind=kOutput, calls=%fused_computation | convolution fusion | flops 6442975232 | bytes 10485760 | tf_op jit(solution)/shard_map/dot_general | solution.py:8
Async XLA Ops:
  6.5 15.7 %all-gather.5.cloned.1.call-start = ((), (), s32[]{:S(2)}) async-start(), calls=%async_computation.1 | async-start | bytes 3145728 | tf_op jit(solution)/shard_map/all_gather | solution.py:20
  7.3 95.0 %all-gather.3.cloned.1.call-start = ((), (), s32[]{:S(2)}) async-start(), calls=%async_computation | async-start | bytes 4456448 | tf_op jit(solution)/shard_map/all_gather | solution.py:19
Sparse Core Ops, SparseCore 0:
  8.9 13.2 all-gather.4
  25.0 77.2 all-gather.2
where the time goes:
time: 126 us
  waiting for transfers between devices  93.9 us (75%)
  matrix products  16.9 us (13%)
  between operations  13.4 us (11%)
  other arithmetic  1.75 us (1%)
    all_gather x1, waiting for transfers between devices, local(): rows_all = lax.all_gather(scaled, 'col', axis=1, tiled=True)  80.1 us
    dot_general x1, matrix products, outer_modes(): lax.dot_general(left, right, (((1,), (1,)), ((), ())), precision=lax.Prec...  16.9 us
    all_gather x1, waiting for transfers between devices, local(): cols_all = lax.all_gather(phi_cols, 'row', axis=1, tiled=True)  13.1 us
  transfers between devices with their start and end apart: 2, of which 2 were waited for; matrix products, arithmetic and copies ran while one was open for 1% of the time, Pallas kernels for 0%

commit v1 on v0

v1 whole, which is shorter than its diff:
```python
import functools

import jax
import jax.numpy as jnp
from jax import lax
from jax.experimental import pallas as pl
from jax.experimental.pallas import tpu as pltpu
from jax.sharding import PartitionSpec as P

BF16, F32 = jnp.bfloat16, jnp.float32


def moves(layers):
    def perm(target):
        pairs = []
        for z in range(layers):
            for y in range(2):
                for x in range(2):
                    for core in range(2):
                        tz, ty, tx = target(z, y, x, core)
                        pairs.append((((z * 2 + y) * 2 + x) * 2 + core, ((tz * 2 + ty) * 2 + tx) * 2 + core))
        return pairs

    first = perm(lambda z, y, x, core: (z, y, 1 - x) if core == 0 else (z, 1 - y, x))
    second = perm(lambda z, y, x, core: (z, 1 - y, x) if core == 0 else (z, y, 1 - x))
    layer = [perm(lambda z, y, x, core: (z ^ step, y, x)) for step in range(layers)]
    return first, second, layer


def send(value, pairs):
    return lax.ppermute(value, ("col", "row"), pairs)


def after(value, *earlier):
    return lax.optimization_barrier((value, *earlier))[0]


def gather_layers(own):
    first, second, layer = moves(4)
    m = own.shape[0]
    near = send(own, layer[1])
    own_a = send(own, first)
    far = send(own, layer[2])
    own_b = send(own, second)
    pair = send(after(jnp.concatenate([own_a, near]), own_b), second)
    near_a = send(near, first)
    last = send(far, layer[1])
    far_a = send(after(far, near_a), first)
    pair2 = send(after(jnp.concatenate([near_a, far]), pair), second)
    last_a = send(after(last, far_a), first)
    pair3 = send(after(jnp.concatenate([far_a, last]), pair2), second)
    last_d = send(last_a, second)
    return (
        (own, own_a, own_b, pair[:m]),
        (near, near_a, pair[m:], pair2[:m]),
        (far, far_a, pair2[m:], pair3[:m]),
        (last, last_a, pair3[m:], last_d),
    )


def split(value):
    high = value.astype(BF16)
    return high, (value - high.astype(F32)).astype(BF16)


def prepare_kernel(mine_ref, other_ref, high_ref, low_ref, turned):
    col, core = lax.axis_index("col"), lax.axis_index("row")
    layers, depth, _ = high_ref.shape
    m = depth // 4
    half = mine_ref.shape[1] // depth
    z, y, x = col // 4, (col // 2) % 2, col % 2
    ahead = jnp.where(core == 0, 1, 2)
    place = y * 2 + x
    for step in range(layers):
        at = z ^ step
        start = pl.multiple_of((at % half) * depth, depth)

        @pl.when(at // half == core)
        def _():
            turned[...] = mine_ref[:, pl.ds(start, depth)].T

        @pl.when(at // half != core)
        def _():
            turned[...] = other_ref[:, pl.ds(start, depth)].T

        for slot, bits in enumerate((0, ahead, 3 - ahead, 3)):
            block = turned[pl.ds(pl.multiple_of((place ^ bits) * m, m), m), :]
            high, low = split(block)
            high_ref[step, slot * m : (slot + 1) * m, :] = high
            low_ref[step, slot * m : (slot + 1) * m, :] = low


def prepare(mine, other, layers):
    cols, modes = mine.shape
    depth = modes * 2 // layers
    shape = jax.ShapeDtypeStruct((layers, depth, cols), BF16)
    return pl.pallas_call(
        prepare_kernel,
        out_shape=(shape, shape),
        in_specs=[pl.BlockSpec(memory_space=pltpu.VMEM)] * 2,
        out_specs=[pl.BlockSpec(memory_space=pltpu.VMEM)] * 2,
        scratch_shapes=[pltpu.VMEM((depth, cols), F32)],
        compiler_params=pltpu.CompilerParams(vmem_limit_bytes=24 << 20),
        cost_estimate=pl.CostEstimate(flops=0, bytes_accessed=8 * cols * modes * 2, transcendentals=0),
        name="prepare_cols",
    )(mine, other)


def layer_kernel(*refs):
    *unit_refs, high_ref, low_ref, total_ref, out_ref = refs
    left = jnp.concatenate([ref[...] for ref in unit_refs], axis=0).T
    left_high, left_low = split(left)
    dot = functools.partial(jnp.dot, preferred_element_type=F32)
    update = dot(left_high, high_ref[0]) + (dot(left_high, low_ref[0]) + dot(left_low, high_ref[0]))
    out_ref[...] = total_ref[...] - update


def subtract_layer(total, units, high, low, step, tile=256):
    rows, cols = total.shape
    m, depth = units[0].shape[0], high.shape[1]
    cols_spec = pl.BlockSpec((1, depth, cols), lambda i: (step, 0, 0))
    return pl.pallas_call(
        layer_kernel,
        grid=(rows // tile,),
        out_shape=jax.ShapeDtypeStruct((rows, cols), F32),
        in_specs=[pl.BlockSpec((m, tile), lambda i: (0, i))] * 4 + [cols_spec] * 2 + [pl.BlockSpec((tile, cols), lambda i: (i, 0))],
        out_specs=pl.BlockSpec((tile, cols), lambda i: (i, 0)),
        compiler_params=pltpu.CompilerParams(vmem_limit_bytes=24 << 20),
        cost_estimate=pl.CostEstimate(flops=6 * rows * cols * depth, bytes_accessed=8 * rows * cols, transcendentals=0),
        name="subtract_layer",
    )(*units, high, low, total)


def local_by_layers(static_flex, phi_slab, phi_cols, eigenvalues):
    other = lax.ppermute(phi_cols, "row", [(0, 1), (1, 0)])
    scaled = phi_slab.T / eigenvalues[:, None]
    layers = gather_layers(scaled)
    high, low = prepare(phi_cols, other, len(layers))
    total = static_flex
    for step, units in enumerate(layers):
        total = subtract_layer(total, units, high, low, step)
    return total


def local_by_all_gather(static_flex, phi_slab, phi_cols, eigenvalues):
    scaled = phi_slab / eigenvalues[None, :]
    rows_all = lax.all_gather(scaled, "col", axis=1, tiled=True)
    cols_all = lax.all_gather(phi_cols, "row", axis=1, tiled=True)
    update = lax.dot_general(
        rows_all, cols_all, (((1,), (1,)), ((), ())), precision=lax.Precision.HIGHEST, preferred_element_type=F32
    )
    return static_flex - update


def solution(mesh):
    placed = (P("row", "col"), P("row", "col"), P("col", "row"), P("col"))
    four_layers = mesh.shape["col"] == 16 and mesh.shape["row"] == 2
    local = local_by_layers if four_layers else local_by_all_gather
    return jax.shard_map(local, mesh=mesh, in_specs=placed, out_specs=P("row", "col"), check_vma=False)
```

time: 126 us -> 57.6 us (0.46)
  waiting for transfers between devices: 93.9 us -> 32.4 us
  matrix products: 16.9 us -> 0 us
  starting transfers between devices: 0.04 us -> 14 us
  between operations: 13.4 us -> 0.17 us
  Pallas kernels: 0 us -> 9.58 us
    all_gather x2 -> x0, waiting for transfers between devices: 93.2 us -> none  [the longest x1 80.1 us: local(): rows_all = lax.all_gather(scaled, 'col', axis=1, tiled=True)]
    ppermute x0 -> x13, waiting for transfers between devices: none -> 32.4 us  [the longest x12 32.4 us: send(): return lax.ppermute(value, ('col', 'row'), pairs)]
    dot_general x1 -> x0, matrix products: 16.9 us -> none  [outer_modes(): lax.dot_general(left, right, (((1,), (1,)), ((), ())), precision=lax.Prec...]
    ppermute x0 -> x13, starting transfers between devices: none -> 14 us  [the longest x12 14 us: send(): return lax.ppermute(value, ('col', 'row'), pairs)]
    pallas_call x0 -> x5, Pallas kernels: none -> 9.58 us  [the longest x4 8.5 us: subtract_layer(): pl.pallas_call(layer_kernel, grid=(rows // tile,), out_shape=jax.ShapeDty...]
  transfers between devices with their start and end apart: 2 -> 13, of which waited for: 2 -> 7; matrix products, arithmetic and copies ran while one was open for 1% -> 0% of each run, Pallas kernels for 0% -> 12%
where the time goes in v1:
time: 57.6 us; the launch traced here: 57.4 us
  waiting for transfers between devices  32.4 us (56%)
  starting transfers between devices  14 us (24%)
  Pallas kernels  9.58 us (17%)
  other arithmetic  1.16 us (2%)
    ppermute x12, waiting for transfers between devices, send(): return lax.ppermute(value, ('col', 'row'), pairs)  32.4 us
    ppermute x12, starting transfers between devices, send(): return lax.ppermute(value, ('col', 'row'), pairs)  14 us
    pallas_call x4, Pallas kernels, subtract_layer(): pl.pallas_call(layer_kernel, grid=(rows // tile,), out_shape=jax.ShapeDty...  8.5 us
  transfers between devices with their start and end apart: 13, of which 7 were waited for; matrix products, arithmetic and copies ran while one was open for 0% of the time, Pallas kernels for 12%

profile of v1, /device:TPU:0, one launch (start us, length us, event | category | flops | bytes accessed | tf_op | source)
XLA Modules:
  0.0 57.4 jit_solution(3613695863168079864)
XLA Ops:
  0.0 1.0 %divide_bitcast_fusion.refs_0_ = f32[64,1024]{1,0:T(8,128)S(1)} fusion(f32[1024,64]{0,1:T(8,128)} %param.5, f32[64]{0:T(128)} %param.7), kind=kLoop, calls=%fused_computation.3 | loop fusion | flops 65536 | bytes 524544 | tf_op jit(solution)/shard_map/div | solution.py:136
  1.0 0.0 copy-start.1
  1.1 3.1 %collective-permute-start.2 = (f32[64,1024]{1,0:T(8,128)S(1)}, f32[64,1024]{1,0:T(8,128)S(1)}, u32[]{:S(2)}, u32[]{:S(2)}) collective-permute-start(f32[64,1024]{1,0:T(8,128)S(1)} %divide_bitcast_fusion.refs_0_), channel_id=1, source_target_pairs={{0,8},{1,9},{2,10},{3,11},{4,12},{5,13},{6,14},{7,15},{8,0},{9,1},... | collective-permute-start | bytes 786440 | tf_op jit(solution)/shard_map/ppermute | solution.py:31
  4.1 1.5 %collective-permute-start.6 = (f32[64,1024]{1,0:T(8,128)S(1)}, f32[64,1024]{1,0:T(8,128)S(1)}, u32[]{:S(2)}, u32[]{:S(2)}) collective-permute-start(f32[64,1024]{1,0:T(8,128)S(1)} %divide_bitcast_fusion.refs_0_), channel_id=1, source_target_pairs={{0,2},{1,5},{2,0},{3,7},{4,6},{5,1},{6,4},{7,3},{8,10},{9,13},{10,... | collective-permute-start | bytes 786440 | tf_op jit(solution)/shard_map/ppermute | solution.py:31
  5.6 1.5 %collective-permute-start.7 = (f32[64,1024]{1,0:T(8,128)S(1)}, f32[64,1024]{1,0:T(8,128)S(1)}, u32[]{:S(2)}, u32[]{:S(2)}) collective-permute-start(f32[64,1024]{1,0:T(8,128)S(1)} %divide_bitcast_fusion.refs_0_), channel_id=1, source_target_pairs={{0,4},{1,3},{2,6},{3,1},{4,0},{5,7},{6,2},{7,5},{8,12},{9,11},{10,... | collective-permute-start | bytes 786440 | tf_op jit(solution)/shard_map/ppermute | solution.py:31
  7.2 3.3 %collective-permute-done.2.refs_0_ = f32[64,1024]{1,0:T(8,128)S(1)} collective-permute-done((f32[64,1024]{1,0:T(8,128)S(1)}, f32[64,1024]{1,0:T(8,128)S(1)}, u32[]{:S(2)}, u32[]{:S(2)}) %collective-permute-start.2) | collective-permute-done | bytes 262176 | tf_op jit(solution)/shard_map/ppermute | solution.py:31
  10.5 2.7 %collective-permute-done.6.refs_1_ = f32[64,1024]{1,0:T(8,128)S(1)} collective-permute-done((f32[64,1024]{1,0:T(8,128)S(1)}, f32[64,1024]{1,0:T(8,128)S(1)}, u32[]{:S(2)}, u32[]{:S(2)}) %collective-permute-start.6) | collective-permute-done | bytes 262176 | tf_op jit(solution)/shard_map/ppermute | solution.py:31
  13.2 0.0 collective-permute-done.7.refs_2_
  13.2 0.6 collective-permute-start.8
  13.8 2.6 %collective-permute-start = (f32[64,1024]{1,0:T(8,128)S(1)}, f32[64,1024]{1,0:T(8,128)S(1)}, u32[]{:S(2)}, u32[]{:S(2)}) collective-permute-start(f32[64,1024]{1,0:T(8,128)S(1)} %divide_bitcast_fusion.refs_0_), channel_id=1, source_target_pairs={{0,16},{1,17},{2,18},{3,19},{4,20},{5,21},{6,22},{7,23},{8,24},{9,... | collective-permute-start | bytes 786440 | tf_op jit(solution)/shard_map/ppermute | solution.py:31
  16.4 1.5 %collective-permute-start.3 = (f32[64,1024]{1,0:T(8,128)S(1)}, f32[64,1024]{1,0:T(8,128)S(1)}, u32[]{:S(2)}, u32[]{:S(2)}) collective-permute-start(f32[64,1024]{1,0:T(8,128)S(1)} %collective-permute-done.2.refs_0_), channel_id=1, source_target_pairs={{0,2},{1,5},{2,0},{3,7},{4,6},{5,1},{6,4},{7,3},{8,10},{9,13},{10,... | collective-permute-start | bytes 786440 | tf_op jit(solution)/shard_map/ppermute | solution.py:31
  17.9 0.0 collective-permute-start.12
  17.9 11.1 %collective-permute-done.refs_0_ = f32[64,1024]{1,0:T(8,128)S(1)} collective-permute-done((f32[64,1024]{1,0:T(8,128)S(1)}, f32[64,1024]{1,0:T(8,128)S(1)}, u32[]{:S(2)}, u32[]{:S(2)}) %collective-permute-start) | collective-permute-done | bytes 262176 | tf_op jit(solution)/shard_map/ppermute | solution.py:31
  28.9 0.0 collective-permute-done.3.refs_1_
  29.0 0.0 copy-start
  29.0 0.0 collective-permute-done.8
  29.0 0.1 collective-permute-start.9
  29.1 0.1 collective-permute-start.1
  29.2 0.5 collective-permute-start.4
  29.7 7.8 %collective-permute-done.1.refs_0_ = f32[64,1024]{1,0:T(8,128)S(1)} collective-permute-done((f32[64,1024]{1,0:T(8,128)S(1)}, f32[64,1024]{1,0:T(8,128)S(1)}, u32[]{:S(2)}, u32[]{:S(2)}) %collective-permute-start.1) | collective-permute-done | bytes 262176 | tf_op jit(solution)/shard_map/ppermute | solution.py:31
  37.5 0.9 %collective-permute-done.4.refs_1_ = f32[64,1024]{1,0:T(8,128)S(1)} collective-permute-done((f32[64,1024]{1,0:T(8,128)S(1)}, f32[64,1024]{1,0:T(8,128)S(1)}, u32[]{:S(2)}, u32[]{:S(2)}) %collective-permute-start.4) | collective-permute-done | bytes 262176 | tf_op jit(solution)/shard_map/ppermute | solution.py:31
  38.4 0.5 collective-permute-start.5
  38.9 2.1 %collective-permute-done.9 = f32[128,1024]{1,0:T(8,128)S(1)} collective-permute-done((f32[128,1024]{1,0:T(8,128)S(1)}, f32[128,1024]{1,0:T(8,128)S(1)}, u32[]{:S(2)}, u32[]{:S(2)}) %collective-permute-start.9) | collective-permute-done | bytes 524320 | tf_op jit(solution)/shard_map/ppermute | solution.py:31
  41.1 0.0 collective-permute-start.10
  41.1 0.0 collective-permute-done.12.other_ref
  41.1 0.0 copy-done.1
  41.1 1.1 %prepare_cols.1 = (bf16[4,256,512]{2,1,0:T(8,128)(2,1)S(1)}, bf16[4,256,512]{2,1,0:T(8,128)(2,1)S(1)}) custom-call(f32[512,512]{1,0:T(8,128)S(1)} %copy-done.1, f32[512,512]{1,0:T(8,128)S(1)} %collective-permute-done.12.other_ref), custom_call_target="tpu_custom_call" | custom-call | bytes 4194304 | tf_op jit(solution)/shard_map/prepare_cols/pallas_call | solution.py:97
  42.2 4.5 %collective-permute-done.5.refs_1_ = f32[64,1024]{1,0:T(8,128)S(1)} collective-permute-done((f32[64,1024]{1,0:T(8,128)S(1)}, f32[64,1024]{1,0:T(8,128)S(1)}, u32[]{:S(2)}, u32[]{:S(2)}) %collective-permute-start.5) | collective-permute-done | bytes 262176 | tf_op jit(solution)/shard_map/ppermute | solution.py:31
  46.7 2.1 %collective-permute-start.11 = (f32[64,1024]{1,0:T(8,128)S(1)}, f32[64,1024]{1,0:T(8,128)S(1)}, u32[]{:S(2)}, u32[]{:S(2)}) collective-permute-start(f32[64,1024]{1,0:T(8,128)S(1)} %collective-permute-done.5.refs_1_), channel_id=1, source_target_pairs={{0,4},{1,3},{2,6},{3,1},{4,0},{5,7},{6,2},{7,5},{8,12},{9,11},{10,... | collective-permute-start | bytes 786440 | tf_op jit(solution)/shard_map/ppermute | solution.py:31
  48.8 0.0 copy-done
  48.8 1.8 %subtract_layer.4.refs_6_ = f32[1024,512]{1,0:T(8,128)S(1)} custom-call(f32[64,1024]{1,0:T(8,128)S(1)} %divide_bitcast_fusion.refs_0_, f32[64,1024]{1,0:T(8,128)S(1)} %collective-permute-done.6.refs_1_, f32[64,1024]{1,0:T(8,128)S(1)} %collective-permute-done.7.refs_2_, f32[64,1024]{1,0:T(8,128)S(1)} %get-tuple-element.19.refs_3_, ...), custom_call_target="tpu_custom_call" | custom-call | flops 805306368 | bytes 4194304 | tf_op jit(solution)/shard_map/subtract_layer/pallas_call | solution.py:122
  50.7 1.8 %subtract_layer.5.refs_6_ = f32[1024,512]{1,0:T(8,128)S(1)} custom-call(f32[64,1024]{1,0:T(8,128)S(1)} %collective-permute-done.2.refs_0_, f32[64,1024]{1,0:T(8,128)S(1)} %collective-permute-done.3.refs_1_, f32[64,1024]{1,0:T(8,128)S(1)} %get-tuple-element.20.refs_2_, f32[64,1024]{1,0:T(8,128)S(1)} %get-tuple-element.21.refs_3_, ...), custom_call_target="tpu_custom_call" | custom-call | flops 805306368 | bytes 4194304 | tf_op jit(solution)/shard_map/subtract_layer/pallas_call | solution.py:122
  52.5 0.0 collective-permute-done.10
  52.6 1.8 %subtract_layer.6.refs_6_ = f32[1024,512]{1,0:T(8,128)S(1)} custom-call(f32[64,1024]{1,0:T(8,128)S(1)} %collective-permute-done.refs_0_, f32[64,1024]{1,0:T(8,128)S(1)} %collective-permute-done.4.refs_1_, f32[64,1024]{1,0:T(8,128)S(1)} %get-tuple-element.22.refs_2_, f32[64,1024]{1,0:T(8,128)S(1)} %get-tuple-element.23.refs_3_, ...), custom_call_target="tpu_custom_call" | custom-call | flops 805306368 | bytes 4194304 | tf_op jit(solution)/shard_map/subtract_layer/pallas_call | solution.py:122
  54.4 0.0 collective-permute-done.11.refs_3_
  54.5 3.0 %subtract_layer.7 = f32[1024,512]{1,0:T(8,128)} custom-call(f32[64,1024]{1,0:T(8,128)S(1)} %collective-permute-done.1.refs_0_, f32[64,1024]{1,0:T(8,128)S(1)} %collective-permute-done.5.refs_1_, f32[64,1024]{1,0:T(8,128)S(1)} %get-tuple-element.24.refs_2_, f32[64,1024]{1,0:T(8,128)S(1)} %collective-permute-done.11.refs_3_, ...), custom_call_target="tpu_custom_call" | custom-call | flops 805306368 | bytes 4194304 | tf_op jit(solution)/shard_map/subtract_layer/pallas_call | solution.py:122
  (6 shorter events, 0.2 us)
Async XLA Ops:
  1.0 40.1 %copy-start.1 = (f32[512,512]{1,0:T(8,128)S(1)}, f32[512,512]{1,0:T(8,128)}, u32[]{:S(2)}) copy-start(f32[512,512]{1,0:T(8,128)} %mine_ref.1) | copy-start | bytes 3145732
  1.1 9.4 %collective-permute-start.2 = (f32[64,1024]{1,0:T(8,128)S(1)}, f32[64,1024]{1,0:T(8,128)S(1)}, u32[]{:S(2)}, u32[]{:S(2)}) collective-permute-start(f32[64,1024]{1,0:T(8,128)S(1)} %divide_bitcast_fusion.refs_0_), channel_id=1, source_target_pairs={{0,8},{1,9},{2,10},{3,11},{4,12},{5,13},{6,14},{7,15},{8,0},{9,1},... | collective-permute-start | bytes 786440 | tf_op jit(solution)/shard_map/ppermute | solution.py:31
  4.1 9.0 %collective-permute-start.6 = (f32[64,1024]{1,0:T(8,128)S(1)}, f32[64,1024]{1,0:T(8,128)S(1)}, u32[]{:S(2)}, u32[]{:S(2)}) collective-permute-start(f32[64,1024]{1,0:T(8,128)S(1)} %divide_bitcast_fusion.refs_0_), channel_id=1, source_target_pairs={{0,2},{1,5},{2,0},{3,7},{4,6},{5,1},{6,4},{7,3},{8,10},{9,13},{10,... | collective-permute-start | bytes 786440 | tf_op jit(solution)/shard_map/ppermute | solution.py:31
  5.6 7.6 %collective-permute-start.7 = (f32[64,1024]{1,0:T(8,128)S(1)}, f32[64,1024]{1,0:T(8,128)S(1)}, u32[]{:S(2)}, u32[]{:S(2)}) collective-permute-start(f32[64,1024]{1,0:T(8,128)S(1)} %divide_bitcast_fusion.refs_0_), channel_id=1, source_target_pairs={{0,4},{1,3},{2,6},{3,1},{4,0},{5,7},{6,2},{7,5},{8,12},{9,11},{10,... | collective-permute-start | bytes 786440 | tf_op jit(solution)/shard_map/ppermute | solution.py:31
  13.2 15.8 %collective-permute-start.8 = (f32[128,1024]{1,0:T(8,128)S(1)}, f32[128,1024]{1,0:T(8,128)S(1)}, u32[]{:S(2)}, u32[]{:S(2)}) collective-permute-start(f32[128,1024]{1,0:T(8,128)S(1)} %pad_maximum_fusion.2), channel_id=1, source_target_pairs={{0,4},{1,3},{2,6},{3,1},{4,0},{5,7},{6,2},{7,5},{8,12},{9,11},{10,... | collective-permute-start | bytes 1572872 | tf_op jit(solution)/shard_map/ppermute | solution.py:31
  13.8 15.1 %collective-permute-start = (f32[64,1024]{1,0:T(8,128)S(1)}, f32[64,1024]{1,0:T(8,128)S(1)}, u32[]{:S(2)}, u32[]{:S(2)}) collective-permute-start(f32[64,1024]{1,0:T(8,128)S(1)} %divide_bitcast_fusion.refs_0_), channel_id=1, source_target_pairs={{0,16},{1,17},{2,18},{3,19},{4,20},{5,21},{6,22},{7,23},{8,24},{9,... | collective-permute-start | bytes 786440 | tf_op jit(solution)/shard_map/ppermute | solution.py:31
  16.4 12.5 %collective-permute-start.3 = (f32[64,1024]{1,0:T(8,128)S(1)}, f32[64,1024]{1,0:T(8,128)S(1)}, u32[]{:S(2)}, u32[]{:S(2)}) collective-permute-start(f32[64,1024]{1,0:T(8,128)S(1)} %collective-permute-done.2.refs_0_), channel_id=1, source_target_pairs={{0,2},{1,5},{2,0},{3,7},{4,6},{5,1},{6,4},{7,3},{8,10},{9,13},{10,... | collective-permute-start | bytes 786440 | tf_op jit(solution)/shard_map/ppermute | solution.py:31
  17.9 23.2 %collective-permute-start.12 = (f32[512,512]{1,0:T(8,128)}, f32[512,512]{1,0:T(8,128)S(1)}, u32[]{:S(2)}, u32[]{:S(2)}) collective-permute-start(f32[512,512]{1,0:T(8,128)} %mine_ref.1), channel_id=1, source_target_pairs={{0,1},{1,0},{2,3},{3,2},{4,5},{5,4},{6,7},{7,6},{8,9},{9,8},{10,11... | collective-permute-start | bytes 3145736 | tf_op jit(solution)/shard_map/ppermute | solution.py:135
  29.0 19.8 %copy-start = (f32[1024,512]{1,0:T(8,128)S(1)}, f32[1024,512]{1,0:T(8,128)}, u32[]{:S(2)}) copy-start(f32[1024,512]{1,0:T(8,128)} %refs_6_.1) | copy-start | bytes 6291460
  29.0 12.1 %collective-permute-start.9 = (f32[128,1024]{1,0:T(8,128)S(1)}, f32[128,1024]{1,0:T(8,128)S(1)}, u32[]{:S(2)}, u32[]{:S(2)}) collective-permute-start(f32[128,1024]{1,0:T(8,128)S(1)} %pad_maximum_fusion.1), channel_id=1, source_target_pairs={{0,4},{1,3},{2,6},{3,1},{4,0},{5,7},{6,2},{7,5},{8,12},{9,11},{10,... | collective-permute-start | bytes 1572872 | tf_op jit(solution)/shard_map/ppermute | solution.py:31
  29.1 8.4 %collective-permute-start.1 = (f32[64,1024]{1,0:T(8,128)S(1)}, f32[64,1024]{1,0:T(8,128)S(1)}, u32[]{:S(2)}, u32[]{:S(2)}) collective-permute-start(f32[64,1024]{1,0:T(8,128)S(1)} %collective-permute-done.refs_0_), channel_id=1, source_target_pairs={{0,8},{1,9},{2,10},{3,11},{4,12},{5,13},{6,14},{7,15},{8,0},{9,1},... | collective-permute-start | bytes 786440 | tf_op jit(solution)/shard_map/ppermute | solution.py:31
  29.2 9.2 %collective-permute-start.4 = (f32[64,1024]{1,0:T(8,128)S(1)}, f32[64,1024]{1,0:T(8,128)S(1)}, u32[]{:S(2)}, u32[]{:S(2)}) collective-permute-start(f32[64,1024]{1,0:T(8,128)S(1)} %collective-permute-done.refs_0_), channel_id=1, source_target_pairs={{0,2},{1,5},{2,0},{3,7},{4,6},{5,1},{6,4},{7,3},{8,10},{9,13},{10,... | collective-permute-start | bytes 786440 | tf_op jit(solution)/shard_map/ppermute | solution.py:31
  38.4 8.3 %collective-permute-start.5 = (f32[64,1024]{1,0:T(8,128)S(1)}, f32[64,1024]{1,0:T(8,128)S(1)}, u32[]{:S(2)}, u32[]{:S(2)}) collective-permute-start(f32[64,1024]{1,0:T(8,128)S(1)} %collective-permute-done.1.refs_0_), channel_id=1, source_target_pairs={{0,2},{1,5},{2,0},{3,7},{4,6},{5,1},{6,4},{7,3},{8,10},{9,13},{10,... | collective-permute-start | bytes 786440 | tf_op jit(solution)/shard_map/ppermute | solution.py:31
  41.1 11.5 %collective-permute-start.10 = (f32[128,1024]{1,0:T(8,128)S(1)}, f32[128,1024]{1,0:T(8,128)S(1)}, u32[]{:S(2)}, u32[]{:S(2)}) collective-permute-start(f32[128,1024]{1,0:T(8,128)S(1)} %pad_maximum_fusion), channel_id=1, source_target_pairs={{0,4},{1,3},{2,6},{3,1},{4,0},{5,7},{6,2},{7,5},{8,12},{9,11},{10,... | collective-permute-start | bytes 1572872 | tf_op jit(solution)/shard_map/ppermute | solution.py:31
  46.7 7.8 %collective-permute-start.11 = (f32[64,1024]{1,0:T(8,128)S(1)}, f32[64,1024]{1,0:T(8,128)S(1)}, u32[]{:S(2)}, u32[]{:S(2)}) collective-permute-start(f32[64,1024]{1,0:T(8,128)S(1)} %collective-permute-done.5.refs_1_), channel_id=1, source_target_pairs={{0,4},{1,3},{2,6},{3,1},{4,0},{5,7},{6,2},{7,5},{8,12},{9,11},{10,... | collective-permute-start | bytes 786440 | tf_op jit(solution)/shard_map/ppermute | solution.py:31

commit v2 on v1

v2 whole, which is shorter than its diff:
```python
import functools

import jax
import jax.numpy as jnp
from jax import lax
from jax.experimental import pallas as pl
from jax.experimental.pallas import tpu as pltpu
from jax.sharding import PartitionSpec as P

BF16, F32 = jnp.bfloat16, jnp.float32


def moves(layers):
    def perm(target):
        pairs = []
        for z in range(layers):
            for y in range(2):
                for x in range(2):
                    for core in range(2):
                        tz, ty, tx = target(z, y, x, core)
                        pairs.append((((z * 2 + y) * 2 + x) * 2 + core, ((tz * 2 + ty) * 2 + tx) * 2 + core))
        return pairs

    first = perm(lambda z, y, x, core: (z, y, 1 - x) if core == 0 else (z, 1 - y, x))
    second = perm(lambda z, y, x, core: (z, 1 - y, x) if core == 0 else (z, y, 1 - x))
    layer = [perm(lambda z, y, x, core: (z ^ step, y, x)) for step in range(layers)]
    return first, second, layer


def send(value, pairs):
    return lax.ppermute(value, ("col", "row"), pairs)


def together(*values):
    return lax.optimization_barrier(values)


ROUNDS = (
    ((0, 0), (0, 1), (1, 0), (0, 2)),
    ((2, 0), (0, 3), (1, 1), (3, 0)),
    ((2, 1), (2, 2), (1, 2), (2, 3)),
    ((1, 3), (3, 1), (3, 2), (3, 3)),
)


def split(value):
    high = value.astype(BF16)
    return high, (value - high.astype(F32)).astype(BF16)


def prepare_kernel(rounds, mine_ref, other_ref, high_ref, low_ref, turned):
    col, core = lax.axis_index("col"), lax.axis_index("row")
    layers, depth, _ = high_ref.shape
    m = depth // 4
    half = mine_ref.shape[1] // depth
    z, y, x = col // 4, (col // 2) % 2, col % 2
    ahead = jnp.where(core == 0, 1, 2)
    place = y * 2 + x
    for step in range(layers):
        at = z ^ step
        start = pl.multiple_of((at % half) * depth, depth)

        @pl.when(at // half == core)
        def _():
            turned[...] = mine_ref[:, pl.ds(start, depth)].T

        @pl.when(at // half != core)
        def _():
            turned[...] = other_ref[:, pl.ds(start, depth)].T

        bits = (0, ahead, 3 - ahead, 3)
        for i, blocks in enumerate(rounds):
            for slot, (layer, seat) in enumerate(blocks):
                if layer == step:
                    block = turned[pl.ds(pl.multiple_of((place ^ bits[seat]) * m, m), m), :]
                    high, low = split(block)
                    high_ref[i, slot * m : (slot + 1) * m, :] = high
                    low_ref[i, slot * m : (slot + 1) * m, :] = low


def prepare(mine, other, rounds):
    layers = len(rounds)
    cols, modes = mine.shape
    depth = modes * 2 // layers
    shape = jax.ShapeDtypeStruct((layers, depth, cols), BF16)
    return pl.pallas_call(
        functools.partial(prepare_kernel, rounds),
        out_shape=(shape, shape),
        in_specs=[pl.BlockSpec(memory_space=pltpu.VMEM)] * 2,
        out_specs=[pl.BlockSpec(memory_space=pltpu.VMEM)] * 2,
        scratch_shapes=[pltpu.VMEM((depth, cols), F32)],
        compiler_params=pltpu.CompilerParams(vmem_limit_bytes=24 << 20),
        cost_estimate=pl.CostEstimate(flops=0, bytes_accessed=8 * cols * modes * 2, transcendentals=0),
        name="prepare_cols",
    )(mine, other)


def update_tile(unit_refs, high, low, rows):
    left = jnp.concatenate([ref[:, rows] for ref in unit_refs], axis=0).T
    left_high, left_low = split(left)
    dot = functools.partial(jnp.dot, preferred_element_type=F32)
    return dot(left_high, high) + (dot(left_high, low) + dot(left_low, high))


def round_kernel(i, tile, *refs):
    *unit_refs, high_ref, low_ref, total_ref, out_ref = refs
    high, low = high_ref[i], low_ref[i]
    for start in range(0, total_ref.shape[0], tile):
        rows = slice(start, start + tile)
        out_ref[rows, :] = total_ref[rows, :] - update_tile(unit_refs, high, low, rows)


def last_kernel(i, tile, *refs):
    *unit_refs, high_ref, low_ref, total_ref, out_ref, done, sems = refs
    high, low = high_ref[i], low_ref[i]
    copies = []
    for slot, start in enumerate(range(0, total_ref.shape[0], tile)):
        rows = slice(start, start + tile)
        done[rows, :] = total_ref[rows, :] - update_tile(unit_refs, high, low, rows)
        copies.append(pltpu.make_async_copy(done.at[pl.ds(start, tile)], out_ref.at[pl.ds(start, tile)], sems.at[slot]))
        copies[-1].start()
    for copy in copies:
        copy.wait()


def subtract_round(total, units, high, low, i, last=False, tile=256):
    rows, cols = total.shape
    depth = high.shape[1]
    in_vmem = pl.BlockSpec(memory_space=pltpu.VMEM)
    scratch = [pltpu.VMEM((rows, cols), F32), pltpu.SemaphoreType.DMA((rows // tile,))] if last else []
    return pl.pallas_call(
        functools.partial(last_kernel if last else round_kernel, i, tile),
        out_shape=jax.ShapeDtypeStruct((rows, cols), F32),
        in_specs=[in_vmem] * (len(units) + 3),
        out_specs=pl.BlockSpec(memory_space=pl.ANY) if last else in_vmem,
        scratch_shapes=scratch,
        compiler_params=pltpu.CompilerParams(vmem_limit_bytes=24 << 20),
        cost_estimate=pl.CostEstimate(flops=6 * rows * cols * depth, bytes_accessed=8 * rows * cols, transcendentals=0),
        name="subtract_last" if last else "subtract_round",
    )(*units, high, low, total)


def local_by_layers(static_flex, phi_slab, phi_cols, eigenvalues):
    first, second, layer = moves(4)
    other = lax.ppermute(phi_cols, "row", [(0, 1), (1, 0)])
    own = phi_slab.T / eigenvalues[:, None]
    own_a = send(own, first)
    near = send(own, layer[1])
    own_b = send(own, second)
    far = send(own, layer[2])
    high, low = prepare(phi_cols, other, ROUNDS)
    own_d = send(own_a, second)
    near_a = send(near, first)
    far, own_d, own_b, high = together(far, own_d, own_b, high)
    last = send(far, layer[1])
    far_a = send(far, first)
    far, near_a = together(far, near_a)
    far_b = send(far, second)
    near_b = send(own_b, layer[1])
    far_d = send(far_a, second)
    near_d = send(near_a, second)
    total = subtract_round(static_flex, (own, own_a, near, own_b), high, low, 0)
    last, total = together(last, total)
    last_a = send(last, first)
    last_b = send(far_b, layer[1])
    last_d = send(last_a, second)
    total = subtract_round(total, (far, own_d, near_a, last), high, low, 1)
    total = subtract_round(total, (far_a, far_b, near_b, far_d), high, low, 2)
    return subtract_round(total, (near_d, last_a, last_b, last_d), high, low, 3, last=True)


def local_by_all_gather(static_flex, phi_slab, phi_cols, eigenvalues):
    scaled = phi_slab / eigenvalues[None, :]
    rows_all = lax.all_gather(scaled, "col", axis=1, tiled=True)
    cols_all = lax.all_gather(phi_cols, "row", axis=1, tiled=True)
    update = lax.dot_general(
        rows_all, cols_all, (((1,), (1,)), ((), ())), precision=lax.Precision.HIGHEST, preferred_element_type=F32
    )
    return static_flex - update


def solution(mesh):
    placed = (P("row", "col"), P("row", "col"), P("col", "row"), P("col"))
    four_layers = mesh.shape["col"] == 16 and mesh.shape["row"] == 2
    local = local_by_layers if four_layers else local_by_all_gather
    return jax.shard_map(local, mesh=mesh, in_specs=placed, out_specs=P("row", "col"), check_vma=False)
```

time: 57.6 us -> 45.4 us (0.79)
  waiting for transfers between devices: 32.4 us -> 17.3 us
  starting transfers between devices: 14 us -> 19.4 us
  Pallas kernels: 9.58 us -> 6.04 us
  local copies, waits for them, and re-layouts: 0.14 us -> 1.23 us
    ppermute x12 -> x15, waiting for transfers between devices: 32.4 us -> 17.3 us  [send(): return lax.ppermute(value, ('col', 'row'), pairs)]
    ppermute x12 -> x15, starting transfers between devices: 14 us -> 18.9 us  [send(): return lax.ppermute(value, ('col', 'row'), pairs)]
    pallas_call x5, Pallas kernels: 9.58 us -> 6.04 us  [the longest x4 4.99 us: subtract_round(): pl.pallas_call(functools.partial(last_kernel if last else round_kernel, i...]
    unnamed x4, local copies, waits for them, and re-layouts: 0.01 us -> 1.23 us
  transfers between devices with their start and end apart: 13 -> 16, of which waited for: 7 -> 7; matrix products, arithmetic and copies ran while one was open for 0% -> 3% of each run, Pallas kernels for 12% -> 9%
where the time goes in v2:
time: 45.4 us; the launch traced here: 45.2 us
  starting transfers between devices  19.4 us (43%)
  waiting for transfers between devices  17.3 us (38%)
  Pallas kernels  6.04 us (13%)
  local copies, waits for them, and re-layouts  1.23 us (3%)
  other arithmetic  1.22 us (3%)
    ppermute x15, starting transfers between devices, send(): return lax.ppermute(value, ('col', 'row'), pairs)  18.9 us
    ppermute x15, waiting for transfers between devices, send(): return lax.ppermute(value, ('col', 'row'), pairs)  17.3 us
    pallas_call x4, Pallas kernels, subtract_round(): pl.pallas_call(functools.partial(last_kernel if last else round_kernel, i...  4.99 us
    unnamed x4, local copies, waits for them, and re-layouts  1.23 us
    div x1, other arithmetic, local_by_layers(): own = phi_slab.T / eigenvalues[:, None]  1.22 us
    pallas_call x1, Pallas kernels, prepare(): pl.pallas_call(functools.partial(prepare_kernel, rounds), out_shape=(shap...  1.05 us
  transfers between devices with their start and end apart: 16, of which 7 were waited for; matrix products, arithmetic and copies ran while one was open for 3% of the time, Pallas kernels for 9%

profile of v2, /device:TPU:0, one launch (start us, length us, event | category | flops | bytes accessed | tf_op | source)
XLA Modules:
  0.0 45.2 jit_solution(13880853898274488066)
XLA Ops:
  0.0 0.0 copy-start
  0.0 0.5 %collective-permute-start.4 = (f32[512,512]{1,0:T(8,128)}, f32[512,512]{1,0:T(8,128)S(1)}, u32[]{:S(2)}, u32[]{:S(2)}) collective-permute-start(f32[512,512]{1,0:T(8,128)} %mine_ref.1), channel_id=1, source_target_pairs={{0,1},{1,0},{2,3},{3,2},{4,5},{5,4},{6,7},{7,6},{8,9},{9,8},{10,11... | collective-permute-start | bytes 3145736 | tf_op jit(solution)/shard_map/ppermute | solution.py:145
  0.5 1.2 %divide_bitcast_fusion.refs_0_ = f32[64,1024]{1,0:T(8,128)S(1)} fusion(f32[1024,64]{0,1:T(8,128)} %param.5, f32[64]{0:T(128)} %param.7), kind=kLoop, calls=%fused_computation | loop fusion | flops 65536 | bytes 524544 | tf_op jit(solution)/shard_map/div | solution.py:146
  1.7 2.5 %collective-permute-start.1 = (f32[64,1024]{1,0:T(8,128)S(1)}, f32[64,1024]{1,0:T(8,128)S(1)}, u32[]{:S(2)}, u32[]{:S(2)}) collective-permute-start(f32[64,1024]{1,0:T(8,128)S(1)} %divide_bitcast_fusion.refs_0_), channel_id=1, source_target_pairs={{0,2},{1,5},{2,0},{3,7},{4,6},{5,1},{6,4},{7,3},{8,10},{9,13},{10,... | collective-permute-start | bytes 786440 | tf_op jit(solution)/shard_map/ppermute | solution.py:31
  4.2 1.6 %collective-permute-start.5 = (f32[64,1024]{1,0:T(8,128)S(1)}, f32[64,1024]{1,0:T(8,128)S(1)}, u32[]{:S(2)}, u32[]{:S(2)}) collective-permute-start(f32[64,1024]{1,0:T(8,128)S(1)} %divide_bitcast_fusion.refs_0_), channel_id=1, source_target_pairs={{0,8},{1,9},{2,10},{3,11},{4,12},{5,13},{6,14},{7,15},{8,0},{9,1},... | collective-permute-start | bytes 786440 | tf_op jit(solution)/shard_map/ppermute | solution.py:31
  5.8 2.6 %collective-permute-start = (f32[64,1024]{1,0:T(8,128)S(1)}, f32[64,1024]{1,0:T(8,128)S(1)}, u32[]{:S(2)}, u32[]{:S(2)}) collective-permute-start(f32[64,1024]{1,0:T(8,128)S(1)} %divide_bitcast_fusion.refs_0_), channel_id=1, source_target_pairs={{0,16},{1,17},{2,18},{3,19},{4,20},{5,21},{6,22},{7,23},{8,24},{9,... | collective-permute-start | bytes 786440 | tf_op jit(solution)/shard_map/ppermute | solution.py:31
  8.4 1.5 %collective-permute-start.3 = (f32[64,1024]{1,0:T(8,128)S(1)}, f32[64,1024]{1,0:T(8,128)S(1)}, u32[]{:S(2)}, u32[]{:S(2)}) collective-permute-start(f32[64,1024]{1,0:T(8,128)S(1)} %divide_bitcast_fusion.refs_0_), channel_id=1, source_target_pairs={{0,4},{1,3},{2,6},{3,1},{4,0},{5,7},{6,2},{7,5},{8,12},{9,11},{10,... | collective-permute-start | bytes 786440 | tf_op jit(solution)/shard_map/ppermute | solution.py:31
  9.9 0.0 collective-permute-done.1.refs_1_
  9.9 0.7 %collective-permute-start.2 = (f32[64,1024]{1,0:T(8,128)S(1)}, f32[64,1024]{1,0:T(8,128)S(1)}, u32[]{:S(2)}, u32[]{:S(2)}) collective-permute-start(f32[64,1024]{1,0:T(8,128)S(1)} %collective-permute-done.1.refs_1_), channel_id=1, source_target_pairs={{0,4},{1,3},{2,6},{3,1},{4,0},{5,7},{6,2},{7,5},{8,12},{9,11},{10,... | collective-permute-start | bytes 786440 | tf_op jit(solution)/shard_map/ppermute | solution.py:31
  10.6 7.4 %collective-permute-done.5.refs_2_ = f32[64,1024]{1,0:T(8,128)S(1)} collective-permute-done((f32[64,1024]{1,0:T(8,128)S(1)}, f32[64,1024]{1,0:T(8,128)S(1)}, u32[]{:S(2)}, u32[]{:S(2)}) %collective-permute-start.5) | collective-permute-done | bytes 262176 | tf_op jit(solution)/shard_map/ppermute | solution.py:31
  18.0 0.4 collective-permute-start.6
  18.4 0.0 collective-permute-done.4.other_ref
  18.4 0.0 copy-start.1
  18.4 1.2 %copy-done.1 = f32[512,512]{1,0:T(8,128)S(1)} copy-done((f32[512,512]{1,0:T(8,128)S(1)}, f32[512,512]{1,0:T(8,128)}, u32[]{:S(2)}) %copy-start.1) | copy-done | bytes 1048600
  19.6 1.1 %prepare_cols.1 = (bf16[4,256,512]{2,1,0:T(8,128)(2,1)S(1)}, bf16[4,256,512]{2,1,0:T(8,128)(2,1)S(1)}) custom-call(f32[512,512]{1,0:T(8,128)S(1)} %copy-done.1, f32[512,512]{1,0:T(8,128)S(1)} %collective-permute-done.4.other_ref), custom_call_target="tpu_custom_call" | custom-call | bytes 4194304 | tf_op jit(solution)/shard_map/prepare_cols/pallas_call | solution.py:86
  20.7 0.0 collective-permute-done.refs_0_
  20.7 0.0 collective-permute-done.3.refs_3_
  20.7 0.0 collective-permute-done.2.refs_1_
  20.7 0.1 collective-permute-start.8
  20.8 1.7 %collective-permute-start.13 = (f32[64,1024]{1,0:T(8,128)S(1)}, f32[64,1024]{1,0:T(8,128)S(1)}, u32[]{:S(2)}, u32[]{:S(2)}) collective-permute-start(f32[64,1024]{1,0:T(8,128)S(1)} %collective-permute-done.refs_0_), channel_id=1, source_target_pairs={{0,2},{1,5},{2,0},{3,7},{4,6},{5,1},{6,4},{7,3},{8,10},{9,13},{10,... | collective-permute-start | bytes 786440 | tf_op jit(solution)/shard_map/ppermute | solution.py:31
  22.5 1.9 %collective-permute-done.6.refs_2_ = f32[64,1024]{1,0:T(8,128)S(1)} collective-permute-done((f32[64,1024]{1,0:T(8,128)S(1)}, f32[64,1024]{1,0:T(8,128)S(1)}, u32[]{:S(2)}, u32[]{:S(2)}) %collective-permute-start.6) | collective-permute-done | bytes 262176 | tf_op jit(solution)/shard_map/ppermute | solution.py:31
  24.4 0.4 collective-permute-start.10
  24.8 0.0 copy-done
  24.8 1.0 %subtract_round.3.refs_6_ = f32[1024,512]{1,0:T(8,128)S(1)} custom-call(f32[64,1024]{1,0:T(8,128)S(1)} %divide_bitcast_fusion.refs_0_, f32[64,1024]{1,0:T(8,128)S(1)} %collective-permute-done.1.refs_1_, f32[64,1024]{1,0:T(8,128)S(1)} %collective-permute-done.5.refs_2_, f32[64,1024]{1,0:T(8,128)S(1)} %collective-permute-done.3.refs_3_, ...), custom_call_target="tpu_custom_call" | custom-call | flops 805306368 | bytes 4194304 | tf_op jit(solution)/shard_map/subtract_round/pallas_call | solution.py:131
  25.8 2.1 %collective-permute-done.8.refs_3_ = f32[64,1024]{1,0:T(8,128)S(1)} collective-permute-done((f32[64,1024]{1,0:T(8,128)S(1)}, f32[64,1024]{1,0:T(8,128)S(1)}, u32[]{:S(2)}, u32[]{:S(2)}) %collective-permute-start.8) | collective-permute-done | bytes 262176 | tf_op jit(solution)/shard_map/ppermute | solution.py:31
  27.9 2.1 %collective-permute-start.9 = (f32[64,1024]{1,0:T(8,128)S(1)}, f32[64,1024]{1,0:T(8,128)S(1)}, u32[]{:S(2)}, u32[]{:S(2)}) collective-permute-start(f32[64,1024]{1,0:T(8,128)S(1)} %collective-permute-done.8.refs_3_), channel_id=1, source_target_pairs={{0,2},{1,5},{2,0},{3,7},{4,6},{5,1},{6,4},{7,3},{8,10},{9,13},{10,... | collective-permute-start | bytes 786440 | tf_op jit(solution)/shard_map/ppermute | solution.py:31
  30.0 0.4 collective-permute-start.14
  30.4 0.0 collective-permute-done.13.refs_0_
  30.4 1.2 %collective-permute-start.15 = (f32[64,1024]{1,0:T(8,128)S(1)}, f32[64,1024]{1,0:T(8,128)S(1)}, u32[]{:S(2)}, u32[]{:S(2)}) collective-permute-start(f32[64,1024]{1,0:T(8,128)S(1)} %collective-permute-done.13.refs_0_), channel_id=1, source_target_pairs={{0,4},{1,3},{2,6},{3,1},{4,0},{5,7},{6,2},{7,5},{8,12},{9,11},{10,... | collective-permute-start | bytes 786440 | tf_op jit(solution)/shard_map/ppermute | solution.py:31
  31.6 0.8 %collective-permute-start.7 = (f32[64,1024]{1,0:T(8,128)S(1)}, f32[64,1024]{1,0:T(8,128)S(1)}, u32[]{:S(2)}, u32[]{:S(2)}) collective-permute-start(f32[64,1024]{1,0:T(8,128)S(1)} %collective-permute-done.6.refs_2_), channel_id=1, source_target_pairs={{0,4},{1,3},{2,6},{3,1},{4,0},{5,7},{6,2},{7,5},{8,12},{9,11},{10,... | collective-permute-start | bytes 786440 | tf_op jit(solution)/shard_map/ppermute | solution.py:31
  32.4 0.6 %collective-permute-done.10.refs_1_ = f32[64,1024]{1,0:T(8,128)S(1)} collective-permute-done((f32[64,1024]{1,0:T(8,128)S(1)}, f32[64,1024]{1,0:T(8,128)S(1)}, u32[]{:S(2)}, u32[]{:S(2)}) %collective-permute-start.10) | collective-permute-done | bytes 262176 | tf_op jit(solution)/shard_map/ppermute | solution.py:31
  33.0 1.1 %collective-permute-start.11 = (f32[64,1024]{1,0:T(8,128)S(1)}, f32[64,1024]{1,0:T(8,128)S(1)}, u32[]{:S(2)}, u32[]{:S(2)}) collective-permute-start(f32[64,1024]{1,0:T(8,128)S(1)} %collective-permute-done.10.refs_1_), channel_id=1, source_target_pairs={{0,8},{1,9},{2,10},{3,11},{4,12},{5,13},{6,14},{7,15},{8,0},{9,1},... | collective-permute-start | bytes 786440 | tf_op jit(solution)/shard_map/ppermute | solution.py:31
  34.1 2.9 %collective-permute-done.9.refs_1_ = f32[64,1024]{1,0:T(8,128)S(1)} collective-permute-done((f32[64,1024]{1,0:T(8,128)S(1)}, f32[64,1024]{1,0:T(8,128)S(1)}, u32[]{:S(2)}, u32[]{:S(2)}) %collective-permute-start.9) | collective-permute-done | bytes 262176 | tf_op jit(solution)/shard_map/ppermute | solution.py:31
  37.0 1.8 %collective-permute-start.12 = (f32[64,1024]{1,0:T(8,128)S(1)}, f32[64,1024]{1,0:T(8,128)S(1)}, u32[]{:S(2)}, u32[]{:S(2)}) collective-permute-start(f32[64,1024]{1,0:T(8,128)S(1)} %collective-permute-done.9.refs_1_), channel_id=1, source_target_pairs={{0,4},{1,3},{2,6},{3,1},{4,0},{5,7},{6,2},{7,5},{8,12},{9,11},{10,... | collective-permute-start | bytes 786440 | tf_op jit(solution)/shard_map/ppermute | solution.py:31
  38.8 1.0 %subtract_round.4.refs_6_ = f32[1024,512]{1,0:T(8,128)S(1)} custom-call(f32[64,1024]{1,0:T(8,128)S(1)} %collective-permute-done.refs_0_, f32[64,1024]{1,0:T(8,128)S(1)} %collective-permute-done.2.refs_1_, f32[64,1024]{1,0:T(8,128)S(1)} %collective-permute-done.6.refs_2_, f32[64,1024]{1,0:T(8,128)S(1)} %collective-permute-done.8.refs_3_, ...), custom_call_target="tpu_custom_call" | custom-call | flops 805306368 | bytes 4194304 | tf_op jit(solution)/shard_map/subtract_round/pallas_call | solution.py:131
  39.9 0.0 collective-permute-done.14.refs_2_
  39.9 0.0 collective-permute-done.15.refs_3_
  39.9 1.0 %subtract_round.5.refs_6_ = f32[1024,512]{1,0:T(8,128)S(1)} custom-call(f32[64,1024]{1,0:T(8,128)S(1)} %collective-permute-done.13.refs_0_, f32[64,1024]{1,0:T(8,128)S(1)} %collective-permute-done.10.refs_1_, f32[64,1024]{1,0:T(8,128)S(1)} %collective-permute-done.14.refs_2_, f32[64,1024]{1,0:T(8,128)S(1)} %collective-permute-done.15.refs_3_, ...), custom_call_target="tpu_custom_call" | custom-call | flops 805306368 | bytes 4194304 | tf_op jit(solution)/shard_map/subtract_round/pallas_call | solution.py:131
  41.0 0.0 collective-permute-done.7.refs_0_
  41.0 0.7 %collective-permute-done.11.refs_2_ = f32[64,1024]{1,0:T(8,128)S(1)} collective-permute-done((f32[64,1024]{1,0:T(8,128)S(1)}, f32[64,1024]{1,0:T(8,128)S(1)}, u32[]{:S(2)}, u32[]{:S(2)}) %collective-permute-start.11) | collective-permute-done | bytes 262176 | tf_op jit(solution)/shard_map/ppermute | solution.py:31
  41.7 1.7 %collective-permute-done.12.refs_3_ = f32[64,1024]{1,0:T(8,128)S(1)} collective-permute-done((f32[64,1024]{1,0:T(8,128)S(1)}, f32[64,1024]{1,0:T(8,128)S(1)}, u32[]{:S(2)}, u32[]{:S(2)}) %collective-permute-start.12) | collective-permute-done | bytes 262176 | tf_op jit(solution)/shard_map/ppermute | solution.py:31
  43.4 1.9 %subtract_last.1 = f32[1024,512]{1,0:T(8,128)} custom-call(f32[64,1024]{1,0:T(8,128)S(1)} %collective-permute-done.7.refs_0_, f32[64,1024]{1,0:T(8,128)S(1)} %collective-permute-done.9.refs_1_, f32[64,1024]{1,0:T(8,128)S(1)} %collective-permute-done.11.refs_2_, f32[64,1024]{1,0:T(8,128)S(1)} %collective-permute-done.12.refs_3_, ...), custom_call_target="tpu_custom_call" | custom-call | flops 805306368 | bytes 4194304 | tf_op jit(solution)/shard_map/subtract_last/pallas_call | solution.py:131
Async XLA Ops:
  0.0 24.8 %copy-start = (f32[1024,512]{1,0:T(8,128)S(1)}, f32[1024,512]{1,0:T(8,128)}, u32[]{:S(2)}) copy-start(f32[1024,512]{1,0:T(8,128)} %refs_6_.1) | copy-start | bytes 6291460
  0.0 18.4 %collective-permute-start.4 = (f32[512,512]{1,0:T(8,128)}, f32[512,512]{1,0:T(8,128)S(1)}, u32[]{:S(2)}, u32[]{:S(2)}) collective-permute-start(f32[512,512]{1,0:T(8,128)} %mine_ref.1), channel_id=1, source_target_pairs={{0,1},{1,0},{2,3},{3,2},{4,5},{5,4},{6,7},{7,6},{8,9},{9,8},{10,11... | collective-permute-start | bytes 3145736 | tf_op jit(solution)/shard_map/ppermute | solution.py:145
  1.7 8.2 %collective-permute-start.1 = (f32[64,1024]{1,0:T(8,128)S(1)}, f32[64,1024]{1,0:T(8,128)S(1)}, u32[]{:S(2)}, u32[]{:S(2)}) collective-permute-start(f32[64,1024]{1,0:T(8,128)S(1)} %divide_bitcast_fusion.refs_0_), channel_id=1, source_target_pairs={{0,2},{1,5},{2,0},{3,7},{4,6},{5,1},{6,4},{7,3},{8,10},{9,13},{10,... | collective-permute-start | bytes 786440 | tf_op jit(solution)/shard_map/ppermute | solution.py:31
  4.2 13.8 %collective-permute-start.5 = (f32[64,1024]{1,0:T(8,128)S(1)}, f32[64,1024]{1,0:T(8,128)S(1)}, u32[]{:S(2)}, u32[]{:S(2)}) collective-permute-start(f32[64,1024]{1,0:T(8,128)S(1)} %divide_bitcast_fusion.refs_0_), channel_id=1, source_target_pairs={{0,8},{1,9},{2,10},{3,11},{4,12},{5,13},{6,14},{7,15},{8,0},{9,1},... | collective-permute-start | bytes 786440 | tf_op jit(solution)/shard_map/ppermute | solution.py:31
  5.8 14.9 %collective-permute-start = (f32[64,1024]{1,0:T(8,128)S(1)}, f32[64,1024]{1,0:T(8,128)S(1)}, u32[]{:S(2)}, u32[]{:S(2)}) collective-permute-start(f32[64,1024]{1,0:T(8,128)S(1)} %divide_bitcast_fusion.refs_0_), channel_id=1, source_target_pairs={{0,16},{1,17},{2,18},{3,19},{4,20},{5,21},{6,22},{7,23},{8,24},{9,... | collective-permute-start | bytes 786440 | tf_op jit(solution)/shard_map/ppermute | solution.py:31
  8.4 12.3 %collective-permute-start.3 = (f32[64,1024]{1,0:T(8,128)S(1)}, f32[64,1024]{1,0:T(8,128)S(1)}, u32[]{:S(2)}, u32[]{:S(2)}) collective-permute-start(f32[64,1024]{1,0:T(8,128)S(1)} %divide_bitcast_fusion.refs_0_), channel_id=1, source_target_pairs={{0,4},{1,3},{2,6},{3,1},{4,0},{5,7},{6,2},{7,5},{8,12},{9,11},{10,... | collective-permute-start | bytes 786440 | tf_op jit(solution)/shard_map/ppermute | solution.py:31
  9.9 10.8 %collective-permute-start.2 = (f32[64,1024]{1,0:T(8,128)S(1)}, f32[64,1024]{1,0:T(8,128)S(1)}, u32[]{:S(2)}, u32[]{:S(2)}) collective-permute-start(f32[64,1024]{1,0:T(8,128)S(1)} %collective-permute-done.1.refs_1_), channel_id=1, source_target_pairs={{0,4},{1,3},{2,6},{3,1},{4,0},{5,7},{6,2},{7,5},{8,12},{9,11},{10,... | collective-permute-start | bytes 786440 | tf_op jit(solution)/shard_map/ppermute | solution.py:31
  18.0 6.4 %collective-permute-start.6 = (f32[64,1024]{1,0:T(8,128)S(1)}, f32[64,1024]{1,0:T(8,128)S(1)}, u32[]{:S(2)}, u32[]{:S(2)}) collective-permute-start(f32[64,1024]{1,0:T(8,128)S(1)} %collective-permute-done.5.refs_2_), channel_id=1, source_target_pairs={{0,2},{1,5},{2,0},{3,7},{4,6},{5,1},{6,4},{7,3},{8,10},{9,13},{10,... | collective-permute-start | bytes 786440 | tf_op jit(solution)/shard_map/ppermute | solution.py:31
  18.4 1.2 %copy-start.1 = (f32[512,512]{1,0:T(8,128)S(1)}, f32[512,512]{1,0:T(8,128)}, u32[]{:S(2)}) copy-start(f32[512,512]{1,0:T(8,128)} %mine_ref.1) | copy-start | bytes 3145732
  20.7 7.2 %collective-permute-start.8 = (f32[64,1024]{1,0:T(8,128)S(1)}, f32[64,1024]{1,0:T(8,128)S(1)}, u32[]{:S(2)}, u32[]{:S(2)}) collective-permute-start(f32[64,1024]{1,0:T(8,128)S(1)} %collective-permute-done.refs_0_), channel_id=1, source_target_pairs={{0,8},{1,9},{2,10},{3,11},{4,12},{5,13},{6,14},{7,15},{8,0},{9,1},... | collective-permute-start | bytes 786440 | tf_op jit(solution)/shard_map/ppermute | solution.py:31
  20.8 9.6 %collective-permute-start.13 = (f32[64,1024]{1,0:T(8,128)S(1)}, f32[64,1024]{1,0:T(8,128)S(1)}, u32[]{:S(2)}, u32[]{:S(2)}) collective-permute-start(f32[64,1024]{1,0:T(8,128)S(1)} %collective-permute-done.refs_0_), channel_id=1, source_target_pairs={{0,2},{1,5},{2,0},{3,7},{4,6},{5,1},{6,4},{7,3},{8,10},{9,13},{10,... | collective-permute-start | bytes 786440 | tf_op jit(solution)/shard_map/ppermute | solution.py:31
  24.4 8.6 %collective-permute-start.10 = (f32[64,1024]{1,0:T(8,128)S(1)}, f32[64,1024]{1,0:T(8,128)S(1)}, u32[]{:S(2)}, u32[]{:S(2)}) collective-permute-start(f32[64,1024]{1,0:T(8,128)S(1)} %collective-permute-done.refs_0_), channel_id=1, source_target_pairs={{0,4},{1,3},{2,6},{3,1},{4,0},{5,7},{6,2},{7,5},{8,12},{9,11},{10,... | collective-permute-start | bytes 786440 | tf_op jit(solution)/shard_map/ppermute | solution.py:31
  27.9 9.1 %collective-permute-start.9 = (f32[64,1024]{1,0:T(8,128)S(1)}, f32[64,1024]{1,0:T(8,128)S(1)}, u32[]{:S(2)}, u32[]{:S(2)}) collective-permute-start(f32[64,1024]{1,0:T(8,128)S(1)} %collective-permute-done.8.refs_3_), channel_id=1, source_target_pairs={{0,2},{1,5},{2,0},{3,7},{4,6},{5,1},{6,4},{7,3},{8,10},{9,13},{10,... | collective-permute-start | bytes 786440 | tf_op jit(solution)/shard_map/ppermute | solution.py:31
  30.0 9.9 %collective-permute-start.14 = (f32[64,1024]{1,0:T(8,128)S(1)}, f32[64,1024]{1,0:T(8,128)S(1)}, u32[]{:S(2)}, u32[]{:S(2)}) collective-permute-start(f32[64,1024]{1,0:T(8,128)S(1)} %collective-permute-done.3.refs_3_), channel_id=1, source_target_pairs={{0,8},{1,9},{2,10},{3,11},{4,12},{5,13},{6,14},{7,15},{8,0},{9,1},... | collective-permute-start | bytes 786440 | tf_op jit(solution)/shard_map/ppermute | solution.py:31
  30.4 9.5 %collective-permute-start.15 = (f32[64,1024]{1,0:T(8,128)S(1)}, f32[64,1024]{1,0:T(8,128)S(1)}, u32[]{:S(2)}, u32[]{:S(2)}) collective-permute-start(f32[64,1024]{1,0:T(8,128)S(1)} %collective-permute-done.13.refs_0_), channel_id=1, source_target_pairs={{0,4},{1,3},{2,6},{3,1},{4,0},{5,7},{6,2},{7,5},{8,12},{9,11},{10,... | collective-permute-start | bytes 786440 | tf_op jit(solution)/shard_map/ppermute | solution.py:31
  31.6 9.3 %collective-permute-start.7 = (f32[64,1024]{1,0:T(8,128)S(1)}, f32[64,1024]{1,0:T(8,128)S(1)}, u32[]{:S(2)}, u32[]{:S(2)}) collective-permute-start(f32[64,1024]{1,0:T(8,128)S(1)} %collective-permute-done.6.refs_2_), channel_id=1, source_target_pairs={{0,4},{1,3},{2,6},{3,1},{4,0},{5,7},{6,2},{7,5},{8,12},{9,11},{10,... | collective-permute-start | bytes 786440 | tf_op jit(solution)/shard_map/ppermute | solution.py:31
  33.0 8.6 %collective-permute-start.11 = (f32[64,1024]{1,0:T(8,128)S(1)}, f32[64,1024]{1,0:T(8,128)S(1)}, u32[]{:S(2)}, u32[]{:S(2)}) collective-permute-start(f32[64,1024]{1,0:T(8,128)S(1)} %collective-permute-done.10.refs_1_), channel_id=1, source_target_pairs={{0,8},{1,9},{2,10},{3,11},{4,12},{5,13},{6,14},{7,15},{8,0},{9,1},... | collective-permute-start | bytes 786440 | tf_op jit(solution)/shard_map/ppermute | solution.py:31
  37.0 6.4 %collective-permute-start.12 = (f32[64,1024]{1,0:T(8,128)S(1)}, f32[64,1024]{1,0:T(8,128)S(1)}, u32[]{:S(2)}, u32[]{:S(2)}) collective-permute-start(f32[64,1024]{1,0:T(8,128)S(1)} %collective-permute-done.9.refs_1_), channel_id=1, source_target_pairs={{0,4},{1,3},{2,6},{3,1},{4,0},{5,7},{6,2},{7,5},{8,12},{9,11},{10,... | collective-permute-start | bytes 786440 | tf_op jit(solution)/shard_map/ppermute | solution.py:31

commit v3 on v2

v3 whole, which is shorter than its diff:
```python
import functools

import jax
import jax.numpy as jnp
from jax import lax
from jax.experimental import pallas as pl
from jax.experimental.pallas import tpu as pltpu
from jax.sharding import PartitionSpec as P

BF16, F32 = jnp.bfloat16, jnp.float32


def moves(layers):
    def perm(target):
        pairs = []
        for z in range(layers):
            for y in range(2):
                for x in range(2):
                    for core in range(2):
                        tz, ty, tx = target(z, y, x, core)
                        pairs.append((((z * 2 + y) * 2 + x) * 2 + core, ((tz * 2 + ty) * 2 + tx) * 2 + core))
        return pairs

    first = perm(lambda z, y, x, core: (z, y, 1 - x) if core == 0 else (z, 1 - y, x))
    second = perm(lambda z, y, x, core: (z, 1 - y, x) if core == 0 else (z, y, 1 - x))
    layer = [perm(lambda z, y, x, core: (z ^ step, y, x)) for step in range(layers)]
    return first, second, layer


def send(value, pairs):
    return lax.ppermute(value, ("col", "row"), pairs)


def together(*values):
    return lax.optimization_barrier(values)


ROUNDS = (
    ((0, 0), (0, 1), (1, 0), (0, 2)),
    ((2, 0), (0, 3), (1, 1), (3, 0)),
    ((2, 1), (2, 2), (1, 2), (2, 3), (1, 3), (3, 1)),
    ((3, 2), (3, 3)),
)


def split(value):
    high = value.astype(BF16)
    return high, (value - high.astype(F32)).astype(BF16)


def prepare_kernel(order, mine_ref, other_ref, high_ref, low_ref, turned):
    col, core = lax.axis_index("col"), lax.axis_index("row")
    depth, m = turned.shape[0], turned.shape[0] // 4
    half = mine_ref.shape[1] // depth
    z, y, x = col // 4, (col // 2) % 2, col % 2
    ahead = jnp.where(core == 0, 1, 2)
    turns = (0, ahead, 3 - ahead, 3)
    for step in range(len(order) // 4):
        at = z ^ step
        start = pl.multiple_of((at % half) * depth, depth)

        @pl.when(at // half == core)
        def _():
            turned[...] = mine_ref[:, pl.ds(start, depth)].T

        @pl.when(at // half != core)
        def _():
            turned[...] = other_ref[:, pl.ds(start, depth)].T

        for i, (layer, seat) in enumerate(order):
            if layer == step:
                block = turned[pl.ds(pl.multiple_of(((y * 2 + x) ^ turns[seat]) * m, m), m), :]
                high_ref[i * m : (i + 1) * m, :], low_ref[i * m : (i + 1) * m, :] = split(block)


def prepare(mine, other, rounds):
    order = [block for blocks in rounds for block in blocks]
    cols, modes = mine.shape
    modes *= 2
    shape = jax.ShapeDtypeStruct((modes, cols), BF16)
    return pl.pallas_call(
        functools.partial(prepare_kernel, order),
        out_shape=(shape, shape),
        in_specs=[pl.BlockSpec(memory_space=pltpu.VMEM)] * 2,
        out_specs=[pl.BlockSpec(memory_space=pltpu.VMEM)] * 2,
        scratch_shapes=[pltpu.VMEM((modes * 4 // len(order), cols), F32)],
        compiler_params=pltpu.CompilerParams(vmem_limit_bytes=24 << 20),
        cost_estimate=pl.CostEstimate(flops=0, bytes_accessed=8 * cols * modes, transcendentals=0),
        name="prepare_cols",
    )(mine, other)


def right_side(high_ref, low_ref, modes):
    high, low = high_ref[modes, :], low_ref[modes, :]
    return jnp.concatenate([high, low, high], axis=0)


def update_tile(unit_refs, right, rows):
    left = jnp.concatenate([ref[:, rows] for ref in unit_refs], axis=0).T
    high, low = split(left)
    return jnp.dot(jnp.concatenate([high, high, low], axis=1), right, preferred_element_type=F32)


def round_kernel(modes, tile, *refs):
    *unit_refs, high_ref, low_ref, total_ref, out_ref = refs
    right = right_side(high_ref, low_ref, modes)
    for start in range(0, total_ref.shape[0], tile):
        rows = slice(start, start + tile)
        out_ref[rows, :] = total_ref[rows, :] - update_tile(unit_refs, right, rows)


def last_kernel(modes, tile, *refs):
    *unit_refs, high_ref, low_ref, total_ref, out_ref, done, sems = refs
    right = right_side(high_ref, low_ref, modes)
    copies = []
    for slot, start in enumerate(range(0, total_ref.shape[0], tile)):
        rows = slice(start, start + tile)
        done[rows, :] = total_ref[rows, :] - update_tile(unit_refs, right, rows)
        copies.append(pltpu.make_async_copy(done.at[pl.ds(start, tile)], out_ref.at[pl.ds(start, tile)], sems.at[slot]))
        copies[-1].start()
    for copy in copies:
        copy.wait()


def subtract_round(total, units, high, low, i):
    last = i == len(ROUNDS) - 1
    tile = 128 if last else 256
    rows, cols = total.shape
    m = units[0].shape[0]
    first = m * sum(len(blocks) for blocks in ROUNDS[:i])
    modes = slice(first, first + m * len(units))
    in_vmem = pl.BlockSpec(memory_space=pltpu.VMEM)
    scratch = [pltpu.VMEM((rows, cols), F32), pltpu.SemaphoreType.DMA((rows // tile,))] if last else []
    return pl.pallas_call(
        functools.partial(last_kernel if last else round_kernel, modes, tile),
        out_shape=jax.ShapeDtypeStruct((rows, cols), F32),
        in_specs=[in_vmem] * (len(units) + 3),
        out_specs=pl.BlockSpec(memory_space=pl.ANY) if last else in_vmem,
        scratch_shapes=scratch,
        compiler_params=pltpu.CompilerParams(vmem_limit_bytes=24 << 20),
        cost_estimate=pl.CostEstimate(flops=6 * rows * cols * m * len(units), bytes_accessed=8 * rows * cols, transcendentals=0),
        name="subtract_last" if last else "subtract_round",
    )(*units, high, low, total)


def local_by_layers(static_flex, phi_slab, phi_cols, eigenvalues):
    first, second, layer = moves(4)
    other = lax.ppermute(phi_cols, "row", [(0, 1), (1, 0)])
    own = phi_slab.T / eigenvalues[:, None]
    own_a = send(own, first)
    near = send(own, layer[1])
    own_b = send(own, second)
    far = send(own, layer[2])
    high, low = prepare(phi_cols, other, ROUNDS)
    own_d = send(own_a, second)
    near_a = send(near, first)
    far, own_b, high = together(far, own_b, high)
    last = send(far, layer[1])
    far_a = send(far, first)
    own_a, far, own_d, own_b, near_a = together(own_a, far, own_d, own_b, near_a)
    far_b = send(far, second)
    near_b = send(own_b, layer[1])
    far_d = send(far_a, second)
    near_d = send(near_a, second)
    total = subtract_round(static_flex, (own, own_a, near, own_b), high, low, 0)
    last, total = together(last, total)
    last_a = send(last, first)
    last_b = send(far_b, layer[1])
    last_d = send(last_a, second)
    total = subtract_round(total, (far, own_d, near_a, last), high, low, 1)
    total = subtract_round(total, (far_a, far_b, near_b, far_d, near_d, last_a), high, low, 2)
    return subtract_round(total, (last_b, last_d), high, low, 3)


def local_by_all_gather(static_flex, phi_slab, phi_cols, eigenvalues):
    scaled = phi_slab / eigenvalues[None, :]
    rows_all = lax.all_gather(scaled, "col", axis=1, tiled=True)
    cols_all = lax.all_gather(phi_cols, "row", axis=1, tiled=True)
    update = lax.dot_general(
        rows_all, cols_all, (((1,), (1,)), ((), ())), precision=lax.Precision.HIGHEST, preferred_element_type=F32
    )
    return static_flex - update


def solution(mesh):
    placed = (P("row", "col"), P("row", "col"), P("col", "row"), P("col"))
    four_layers = mesh.shape["col"] == 16 and mesh.shape["row"] == 2
    local = local_by_layers if four_layers else local_by_all_gather
    return jax.shard_map(local, mesh=mesh, in_specs=placed, out_specs=P("row", "col"), check_vma=False)
```

time: 45.4 us -> 45.2 us (level)
    ppermute x15, waiting for transfers between devices: 17.3 us -> 16.8 us  [send(): return lax.ppermute(value, ('col', 'row'), pairs)]
  transfers between devices with their start and end apart: 16 -> 16, of which waited for: 7 -> 7; matrix products, arithmetic and copies ran while one was open for 3% -> 3% of each run, Pallas kernels for 9% -> 10%
where the time goes in v3:
time: 45.2 us; the launch traced here: 45 us
  starting transfers between devices  19.3 us (43%)
  waiting for transfers between devices  16.9 us (37%)
  Pallas kernels  6.34 us (14%)
  local copies, waits for them, and re-layouts  1.23 us (3%)
  other arithmetic  1.22 us (3%)
    ppermute x15, starting transfers between devices, send(): return lax.ppermute(value, ('col', 'row'), pairs)  18.9 us
    ppermute x15, waiting for transfers between devices, send(): return lax.ppermute(value, ('col', 'row'), pairs)  16.8 us
    pallas_call x4, Pallas kernels, subtract_round(): pl.pallas_call(functools.partial(last_kernel if last else round_kernel, m...  5.28 us
    unnamed x4, local copies, waits for them, and re-layouts  1.23 us
    div x1, other arithmetic, local_by_layers(): own = phi_slab.T / eigenvalues[:, None]  1.22 us
    pallas_call x1, Pallas kernels, prepare(): pl.pallas_call(functools.partial(prepare_kernel, order), out_shape=(shape...  1.05 us
  transfers between devices with their start and end apart: 16, of which 7 were waited for; matrix products, arithmetic and copies ran while one was open for 3% of the time, Pallas kernels for 10%

profile of v3, /device:TPU:0, one launch (start us, length us, event | category | flops | bytes accessed | tf_op | source)
XLA Modules:
  0.0 45.0 jit_solution(6116825140060276292)
XLA Ops:
  0.0 0.0 copy-start
  0.0 0.5 %collective-permute-start.3 = (f32[512,512]{1,0:T(8,128)}, f32[512,512]{1,0:T(8,128)S(1)}, u32[]{:S(2)}, u32[]{:S(2)}) collective-permute-start(f32[512,512]{1,0:T(8,128)} %mine_ref.1), channel_id=1, source_target_pairs={{0,1},{1,0},{2,3},{3,2},{4,5},{5,4},{6,7},{7,6},{8,9},{9,8},{10,11... | collective-permute-start | bytes 3145736 | tf_op jit(solution)/shard_map/ppermute | solution.py:148
  0.5 1.2 %divide_bitcast_fusion.refs_0_ = f32[64,1024]{1,0:T(8,128)S(1)} fusion(f32[1024,64]{0,1:T(8,128)} %param.5, f32[64]{0:T(128)} %param.7), kind=kLoop, calls=%fused_computation | loop fusion | flops 65536 | bytes 524544 | tf_op jit(solution)/shard_map/div | solution.py:149
  1.7 2.5 %collective-permute-start = (f32[64,1024]{1,0:T(8,128)S(1)}, f32[64,1024]{1,0:T(8,128)S(1)}, u32[]{:S(2)}, u32[]{:S(2)}) collective-permute-start(f32[64,1024]{1,0:T(8,128)S(1)} %divide_bitcast_fusion.refs_0_), channel_id=1, source_target_pairs={{0,2},{1,5},{2,0},{3,7},{4,6},{5,1},{6,4},{7,3},{8,10},{9,13},{10,... | collective-permute-start | bytes 786440 | tf_op jit(solution)/shard_map/ppermute | solution.py:31
  4.2 1.6 %collective-permute-start.5 = (f32[64,1024]{1,0:T(8,128)S(1)}, f32[64,1024]{1,0:T(8,128)S(1)}, u32[]{:S(2)}, u32[]{:S(2)}) collective-permute-start(f32[64,1024]{1,0:T(8,128)S(1)} %divide_bitcast_fusion.refs_0_), channel_id=1, source_target_pairs={{0,8},{1,9},{2,10},{3,11},{4,12},{5,13},{6,14},{7,15},{8,0},{9,1},... | collective-permute-start | bytes 786440 | tf_op jit(solution)/shard_map/ppermute | solution.py:31
  5.8 2.6 %collective-permute-start.1 = (f32[64,1024]{1,0:T(8,128)S(1)}, f32[64,1024]{1,0:T(8,128)S(1)}, u32[]{:S(2)}, u32[]{:S(2)}) collective-permute-start(f32[64,1024]{1,0:T(8,128)S(1)} %divide_bitcast_fusion.refs_0_), channel_id=1, source_target_pairs={{0,16},{1,17},{2,18},{3,19},{4,20},{5,21},{6,22},{7,23},{8,24},{9,... | collective-permute-start | bytes 786440 | tf_op jit(solution)/shard_map/ppermute | solution.py:31
  8.4 1.5 %collective-permute-start.2 = (f32[64,1024]{1,0:T(8,128)S(1)}, f32[64,1024]{1,0:T(8,128)S(1)}, u32[]{:S(2)}, u32[]{:S(2)}) collective-permute-start(f32[64,1024]{1,0:T(8,128)S(1)} %divide_bitcast_fusion.refs_0_), channel_id=1, source_target_pairs={{0,4},{1,3},{2,6},{3,1},{4,0},{5,7},{6,2},{7,5},{8,12},{9,11},{10,... | collective-permute-start | bytes 786440 | tf_op jit(solution)/shard_map/ppermute | solution.py:31
  9.9 0.0 collective-permute-done.refs_1_
  9.9 0.7 %collective-permute-start.4 = (f32[64,1024]{1,0:T(8,128)S(1)}, f32[64,1024]{1,0:T(8,128)S(1)}, u32[]{:S(2)}, u32[]{:S(2)}) collective-permute-start(f32[64,1024]{1,0:T(8,128)S(1)} %collective-permute-done.refs_1_), channel_id=1, source_target_pairs={{0,4},{1,3},{2,6},{3,1},{4,0},{5,7},{6,2},{7,5},{8,12},{9,11},{10,... | collective-permute-start | bytes 786440 | tf_op jit(solution)/shard_map/ppermute | solution.py:31
  10.6 7.4 %collective-permute-done.5.refs_2_ = f32[64,1024]{1,0:T(8,128)S(1)} collective-permute-done((f32[64,1024]{1,0:T(8,128)S(1)}, f32[64,1024]{1,0:T(8,128)S(1)}, u32[]{:S(2)}, u32[]{:S(2)}) %collective-permute-start.5) | collective-permute-done | bytes 262176 | tf_op jit(solution)/shard_map/ppermute | solution.py:31
  18.0 0.4 collective-permute-start.6
  18.4 0.0 collective-permute-done.3.other_ref
  18.4 0.0 copy-start.1
  18.4 1.2 %copy-done.1 = f32[512,512]{1,0:T(8,128)S(1)} copy-done((f32[512,512]{1,0:T(8,128)S(1)}, f32[512,512]{1,0:T(8,128)}, u32[]{:S(2)}) %copy-start.1) | copy-done | bytes 1048600
  19.6 1.1 %prepare_cols.1 = (bf16[1024,512]{1,0:T(8,128)(2,1)S(1)}, bf16[1024,512]{1,0:T(8,128)(2,1)S(1)}) custom-call(f32[512,512]{1,0:T(8,128)S(1)} %copy-done.1, f32[512,512]{1,0:T(8,128)S(1)} %collective-permute-done.3.other_ref), custom_call_target="tpu_custom_call" | custom-call | bytes 4194304 | tf_op jit(solution)/shard_map/prepare_cols/pallas_call | solution.py:81
  20.7 0.0 collective-permute-done.1.refs_0_
  20.7 0.0 collective-permute-done.2.refs_3_
  20.7 0.1 collective-permute-start.9
  20.8 1.7 %collective-permute-start.12 = (f32[64,1024]{1,0:T(8,128)S(1)}, f32[64,1024]{1,0:T(8,128)S(1)}, u32[]{:S(2)}, u32[]{:S(2)}) collective-permute-start(f32[64,1024]{1,0:T(8,128)S(1)} %collective-permute-done.1.refs_0_), channel_id=1, source_target_pairs={{0,2},{1,5},{2,0},{3,7},{4,6},{5,1},{6,4},{7,3},{8,10},{9,13},{10,... | collective-permute-start | bytes 786440 | tf_op jit(solution)/shard_map/ppermute | solution.py:31
  22.5 0.0 collective-permute-done.4.refs_1_
  22.5 1.9 %collective-permute-done.6.refs_2_ = f32[64,1024]{1,0:T(8,128)S(1)} collective-permute-done((f32[64,1024]{1,0:T(8,128)S(1)}, f32[64,1024]{1,0:T(8,128)S(1)}, u32[]{:S(2)}, u32[]{:S(2)}) %collective-permute-start.6) | collective-permute-done | bytes 262176 | tf_op jit(solution)/shard_map/ppermute | solution.py:31
  24.4 0.4 collective-permute-start.7
  24.8 0.0 copy-done
  24.8 1.0 %subtract_round.3.refs_6_ = f32[1024,512]{1,0:T(8,128)S(1)} custom-call(f32[64,1024]{1,0:T(8,128)S(1)} %divide_bitcast_fusion.refs_0_, f32[64,1024]{1,0:T(8,128)S(1)} %collective-permute-done.refs_1_, f32[64,1024]{1,0:T(8,128)S(1)} %collective-permute-done.5.refs_2_, f32[64,1024]{1,0:T(8,128)S(1)} %collective-permute-done.2.refs_3_, ...), custom_call_target="tpu_custom_call" | custom-call | flops 805306368 | bytes 4194304 | tf_op jit(solution)/shard_map/subtract_round/pallas_call | solution.py:134
  25.8 2.1 %collective-permute-done.9.refs_3_ = f32[64,1024]{1,0:T(8,128)S(1)} collective-permute-done((f32[64,1024]{1,0:T(8,128)S(1)}, f32[64,1024]{1,0:T(8,128)S(1)}, u32[]{:S(2)}, u32[]{:S(2)}) %collective-permute-start.9) | collective-permute-done | bytes 262176 | tf_op jit(solution)/shard_map/ppermute | solution.py:31
  27.9 2.1 %collective-permute-start.10 = (f32[64,1024]{1,0:T(8,128)S(1)}, f32[64,1024]{1,0:T(8,128)S(1)}, u32[]{:S(2)}, u32[]{:S(2)}) collective-permute-start(f32[64,1024]{1,0:T(8,128)S(1)} %collective-permute-done.9.refs_3_), channel_id=1, source_target_pairs={{0,2},{1,5},{2,0},{3,7},{4,6},{5,1},{6,4},{7,3},{8,10},{9,13},{10,... | collective-permute-start | bytes 786440 | tf_op jit(solution)/shard_map/ppermute | solution.py:31
  30.0 0.4 collective-permute-start.13
  30.4 1.2 %collective-permute-start.15 = (f32[64,1024]{1,0:T(8,128)S(1)}, f32[64,1024]{1,0:T(8,128)S(1)}, u32[]{:S(2)}, u32[]{:S(2)}) collective-permute-start(f32[64,1024]{1,0:T(8,128)S(1)} %collective-permute-done.6.refs_2_), channel_id=1, source_target_pairs={{0,4},{1,3},{2,6},{3,1},{4,0},{5,7},{6,2},{7,5},{8,12},{9,11},{10,... | collective-permute-start | bytes 786440 | tf_op jit(solution)/shard_map/ppermute | solution.py:31
  31.6 0.0 collective-permute-done.12.refs_0_
  31.6 0.8 %collective-permute-start.14 = (f32[64,1024]{1,0:T(8,128)S(1)}, f32[64,1024]{1,0:T(8,128)S(1)}, u32[]{:S(2)}, u32[]{:S(2)}) collective-permute-start(f32[64,1024]{1,0:T(8,128)S(1)} %collective-permute-done.12.refs_0_), channel_id=1, source_target_pairs={{0,4},{1,3},{2,6},{3,1},{4,0},{5,7},{6,2},{7,5},{8,12},{9,11},{10,... | collective-permute-start | bytes 786440 | tf_op jit(solution)/shard_map/ppermute | solution.py:31
  32.4 0.6 %collective-permute-done.7.refs_1_ = f32[64,1024]{1,0:T(8,128)S(1)} collective-permute-done((f32[64,1024]{1,0:T(8,128)S(1)}, f32[64,1024]{1,0:T(8,128)S(1)}, u32[]{:S(2)}, u32[]{:S(2)}) %collective-permute-start.7) | collective-permute-done | bytes 262176 | tf_op jit(solution)/shard_map/ppermute | solution.py:31
  33.0 1.0 %collective-permute-start.8 = (f32[64,1024]{1,0:T(8,128)S(1)}, f32[64,1024]{1,0:T(8,128)S(1)}, u32[]{:S(2)}, u32[]{:S(2)}) collective-permute-start(f32[64,1024]{1,0:T(8,128)S(1)} %collective-permute-done.7.refs_1_), channel_id=1, source_target_pairs={{0,8},{1,9},{2,10},{3,11},{4,12},{5,13},{6,14},{7,15},{8,0},{9,1},... | collective-permute-start | bytes 786440 | tf_op jit(solution)/shard_map/ppermute | solution.py:31
  34.1 2.9 %collective-permute-done.10.refs_5_ = f32[64,1024]{1,0:T(8,128)S(1)} collective-permute-done((f32[64,1024]{1,0:T(8,128)S(1)}, f32[64,1024]{1,0:T(8,128)S(1)}, u32[]{:S(2)}, u32[]{:S(2)}) %collective-permute-start.10) | collective-permute-done | bytes 262176 | tf_op jit(solution)/shard_map/ppermute | solution.py:31
  37.0 1.8 %collective-permute-start.11 = (f32[64,1024]{1,0:T(8,128)S(1)}, f32[64,1024]{1,0:T(8,128)S(1)}, u32[]{:S(2)}, u32[]{:S(2)}) collective-permute-start(f32[64,1024]{1,0:T(8,128)S(1)} %collective-permute-done.10.refs_5_), channel_id=1, source_target_pairs={{0,4},{1,3},{2,6},{3,1},{4,0},{5,7},{6,2},{7,5},{8,12},{9,11},{10,... | collective-permute-start | bytes 786440 | tf_op jit(solution)/shard_map/ppermute | solution.py:31
  38.8 1.0 %subtract_round.4.refs_8_ = f32[1024,512]{1,0:T(8,128)S(1)} custom-call(f32[64,1024]{1,0:T(8,128)S(1)} %collective-permute-done.1.refs_0_, f32[64,1024]{1,0:T(8,128)S(1)} %collective-permute-done.4.refs_1_, f32[64,1024]{1,0:T(8,128)S(1)} %collective-permute-done.6.refs_2_, f32[64,1024]{1,0:T(8,128)S(1)} %collective-permute-done.9.refs_3_, ...), custom_call_target="tpu_custom_call" | custom-call | flops 805306368 | bytes 4194304 | tf_op jit(solution)/shard_map/subtract_round/pallas_call | solution.py:134
  39.9 0.0 collective-permute-done.13.refs_2_
  39.9 0.0 collective-permute-done.15.refs_4_
  39.9 0.0 collective-permute-done.14.refs_3_
  39.9 1.6 %subtract_round.5.refs_4_ = f32[1024,512]{1,0:T(8,128)S(1)} custom-call(f32[64,1024]{1,0:T(8,128)S(1)} %collective-permute-done.12.refs_0_, f32[64,1024]{1,0:T(8,128)S(1)} %collective-permute-done.7.refs_1_, f32[64,1024]{1,0:T(8,128)S(1)} %collective-permute-done.13.refs_2_, f32[64,1024]{1,0:T(8,128)S(1)} %collective-permute-done.14.refs_3_, ...), custom_call_target="tpu_custom_call" | custom-call | flops 1207959552 | bytes 4194304 | tf_op jit(solution)/shard_map/subtract_round/pallas_call | solution.py:134
  41.5 0.2 collective-permute-done.8.refs_0_
  41.7 1.7 %collective-permute-done.11.refs_1_ = f32[64,1024]{1,0:T(8,128)S(1)} collective-permute-done((f32[64,1024]{1,0:T(8,128)S(1)}, f32[64,1024]{1,0:T(8,128)S(1)}, u32[]{:S(2)}, u32[]{:S(2)}) %collective-permute-start.11) | collective-permute-done | bytes 262176 | tf_op jit(solution)/shard_map/ppermute | solution.py:31
  43.4 1.6 %subtract_last.1 = f32[1024,512]{1,0:T(8,128)} custom-call(f32[64,1024]{1,0:T(8,128)S(1)} %collective-permute-done.8.refs_0_, f32[64,1024]{1,0:T(8,128)S(1)} %collective-permute-done.11.refs_1_, bf16[1024,512]{1,0:T(8,128)(2,1)S(1)} %get-tuple-element.23.refs_4_.refs_6_.refs_2_, bf16[1024,512]{1,0:T(8,128)(2,1)S(1)} %get-tuple-element.24.refs_5_.refs_7_.refs_3_, ...), custom_call_target="tpu_custom_call" | custom-call | flops 402653184 | bytes 4194304 | tf_op jit(solution)/shard_map/subtract_last/pallas_call | solution.py:134
Async XLA Ops:
  0.0 24.8 %copy-start = (f32[1024,512]{1,0:T(8,128)S(1)}, f32[1024,512]{1,0:T(8,128)}, u32[]{:S(2)}) copy-start(f32[1024,512]{1,0:T(8,128)} %refs_6_.1) | copy-start | bytes 6291460
  0.0 18.4 %collective-permute-start.3 = (f32[512,512]{1,0:T(8,128)}, f32[512,512]{1,0:T(8,128)S(1)}, u32[]{:S(2)}, u32[]{:S(2)}) collective-permute-start(f32[512,512]{1,0:T(8,128)} %mine_ref.1), channel_id=1, source_target_pairs={{0,1},{1,0},{2,3},{3,2},{4,5},{5,4},{6,7},{7,6},{8,9},{9,8},{10,11... | collective-permute-start | bytes 3145736 | tf_op jit(solution)/shard_map/ppermute | solution.py:148
  1.7 8.2 %collective-permute-start = (f32[64,1024]{1,0:T(8,128)S(1)}, f32[64,1024]{1,0:T(8,128)S(1)}, u32[]{:S(2)}, u32[]{:S(2)}) collective-permute-start(f32[64,1024]{1,0:T(8,128)S(1)} %divide_bitcast_fusion.refs_0_), channel_id=1, source_target_pairs={{0,2},{1,5},{2,0},{3,7},{4,6},{5,1},{6,4},{7,3},{8,10},{9,13},{10,... | collective-permute-start | bytes 786440 | tf_op jit(solution)/shard_map/ppermute | solution.py:31
  4.2 13.8 %collective-permute-start.5 = (f32[64,1024]{1,0:T(8,128)S(1)}, f32[64,1024]{1,0:T(8,128)S(1)}, u32[]{:S(2)}, u32[]{:S(2)}) collective-permute-start(f32[64,1024]{1,0:T(8,128)S(1)} %divide_bitcast_fusion.refs_0_), channel_id=1, source_target_pairs={{0,8},{1,9},{2,10},{3,11},{4,12},{5,13},{6,14},{7,15},{8,0},{9,1},... | collective-permute-start | bytes 786440 | tf_op jit(solution)/shard_map/ppermute | solution.py:31
  5.8 14.9 %collective-permute-start.1 = (f32[64,1024]{1,0:T(8,128)S(1)}, f32[64,1024]{1,0:T(8,128)S(1)}, u32[]{:S(2)}, u32[]{:S(2)}) collective-permute-start(f32[64,1024]{1,0:T(8,128)S(1)} %divide_bitcast_fusion.refs_0_), channel_id=1, source_target_pairs={{0,16},{1,17},{2,18},{3,19},{4,20},{5,21},{6,22},{7,23},{8,24},{9,... | collective-permute-start | bytes 786440 | tf_op jit(solution)/shard_map/ppermute | solution.py:31
  8.4 12.3 %collective-permute-start.2 = (f32[64,1024]{1,0:T(8,128)S(1)}, f32[64,1024]{1,0:T(8,128)S(1)}, u32[]{:S(2)}, u32[]{:S(2)}) collective-permute-start(f32[64,1024]{1,0:T(8,128)S(1)} %divide_bitcast_fusion.refs_0_), channel_id=1, source_target_pairs={{0,4},{1,3},{2,6},{3,1},{4,0},{5,7},{6,2},{7,5},{8,12},{9,11},{10,... | collective-permute-start | bytes 786440 | tf_op jit(solution)/shard_map/ppermute | solution.py:31
  9.9 12.6 %collective-permute-start.4 = (f32[64,1024]{1,0:T(8,128)S(1)}, f32[64,1024]{1,0:T(8,128)S(1)}, u32[]{:S(2)}, u32[]{:S(2)}) collective-permute-start(f32[64,1024]{1,0:T(8,128)S(1)} %collective-permute-done.refs_1_), channel_id=1, source_target_pairs={{0,4},{1,3},{2,6},{3,1},{4,0},{5,7},{6,2},{7,5},{8,12},{9,11},{10,... | collective-permute-start | bytes 786440 | tf_op jit(solution)/shard_map/ppermute | solution.py:31
  18.0 6.4 %collective-permute-start.6 = (f32[64,1024]{1,0:T(8,128)S(1)}, f32[64,1024]{1,0:T(8,128)S(1)}, u32[]{:S(2)}, u32[]{:S(2)}) collective-permute-start(f32[64,1024]{1,0:T(8,128)S(1)} %collective-permute-done.5.refs_2_), channel_id=1, source_target_pairs={{0,2},{1,5},{2,0},{3,7},{4,6},{5,1},{6,4},{7,3},{8,10},{9,13},{10,... | collective-permute-start | bytes 786440 | tf_op jit(solution)/shard_map/ppermute | solution.py:31
  18.4 1.2 %copy-start.1 = (f32[512,512]{1,0:T(8,128)S(1)}, f32[512,512]{1,0:T(8,128)}, u32[]{:S(2)}) copy-start(f32[512,512]{1,0:T(8,128)} %mine_ref.1) | copy-start | bytes 3145732
  20.7 7.2 %collective-permute-start.9 = (f32[64,1024]{1,0:T(8,128)S(1)}, f32[64,1024]{1,0:T(8,128)S(1)}, u32[]{:S(2)}, u32[]{:S(2)}) collective-permute-start(f32[64,1024]{1,0:T(8,128)S(1)} %collective-permute-done.1.refs_0_), channel_id=1, source_target_pairs={{0,8},{1,9},{2,10},{3,11},{4,12},{5,13},{6,14},{7,15},{8,0},{9,1},... | collective-permute-start | bytes 786440 | tf_op jit(solution)/shard_map/ppermute | solution.py:31
  20.8 10.8 %collective-permute-start.12 = (f32[64,1024]{1,0:T(8,128)S(1)}, f32[64,1024]{1,0:T(8,128)S(1)}, u32[]{:S(2)}, u32[]{:S(2)}) collective-permute-start(f32[64,1024]{1,0:T(8,128)S(1)} %collective-permute-done.1.refs_0_), channel_id=1, source_target_pairs={{0,2},{1,5},{2,0},{3,7},{4,6},{5,1},{6,4},{7,3},{8,10},{9,13},{10,... | collective-permute-start | bytes 786440 | tf_op jit(solution)/shard_map/ppermute | solution.py:31
  24.4 8.6 %collective-permute-start.7 = (f32[64,1024]{1,0:T(8,128)S(1)}, f32[64,1024]{1,0:T(8,128)S(1)}, u32[]{:S(2)}, u32[]{:S(2)}) collective-permute-start(f32[64,1024]{1,0:T(8,128)S(1)} %collective-permute-done.1.refs_0_), channel_id=1, source_target_pairs={{0,4},{1,3},{2,6},{3,1},{4,0},{5,7},{6,2},{7,5},{8,12},{9,11},{10,... | collective-permute-start | bytes 786440 | tf_op jit(solution)/shard_map/ppermute | solution.py:31
  27.9 9.1 %collective-permute-start.10 = (f32[64,1024]{1,0:T(8,128)S(1)}, f32[64,1024]{1,0:T(8,128)S(1)}, u32[]{:S(2)}, u32[]{:S(2)}) collective-permute-start(f32[64,1024]{1,0:T(8,128)S(1)} %collective-permute-done.9.refs_3_), channel_id=1, source_target_pairs={{0,2},{1,5},{2,0},{3,7},{4,6},{5,1},{6,4},{7,3},{8,10},{9,13},{10,... | collective-permute-start | bytes 786440 | tf_op jit(solution)/shard_map/ppermute | solution.py:31
  30.0 9.9 %collective-permute-start.13 = (f32[64,1024]{1,0:T(8,128)S(1)}, f32[64,1024]{1,0:T(8,128)S(1)}, u32[]{:S(2)}, u32[]{:S(2)}) collective-permute-start(f32[64,1024]{1,0:T(8,128)S(1)} %collective-permute-done.2.refs_3_), channel_id=1, source_target_pairs={{0,8},{1,9},{2,10},{3,11},{4,12},{5,13},{6,14},{7,15},{8,0},{9,1},... | collective-permute-start | bytes 786440 | tf_op jit(solution)/shard_map/ppermute | solution.py:31
  30.4 9.5 %collective-permute-start.15 = (f32[64,1024]{1,0:T(8,128)S(1)}, f32[64,1024]{1,0:T(8,128)S(1)}, u32[]{:S(2)}, u32[]{:S(2)}) collective-permute-start(f32[64,1024]{1,0:T(8,128)S(1)} %collective-permute-done.6.refs_2_), channel_id=1, source_target_pairs={{0,4},{1,3},{2,6},{3,1},{4,0},{5,7},{6,2},{7,5},{8,12},{9,11},{10,... | collective-permute-start | bytes 786440 | tf_op jit(solution)/shard_map/ppermute | solution.py:31
  31.6 8.3 %collective-permute-start.14 = (f32[64,1024]{1,0:T(8,128)S(1)}, f32[64,1024]{1,0:T(8,128)S(1)}, u32[]{:S(2)}, u32[]{:S(2)}) collective-permute-start(f32[64,1024]{1,0:T(8,128)S(1)} %collective-permute-done.12.refs_0_), channel_id=1, source_target_pairs={{0,4},{1,3},{2,6},{3,1},{4,0},{5,7},{6,2},{7,5},{8,12},{9,11},{10,... | collective-permute-start | bytes 786440 | tf_op jit(solution)/shard_map/ppermute | solution.py:31
  33.0 8.6 %collective-permute-start.8 = (f32[64,1024]{1,0:T(8,128)S(1)}, f32[64,1024]{1,0:T(8,128)S(1)}, u32[]{:S(2)}, u32[]{:S(2)}) collective-permute-start(f32[64,1024]{1,0:T(8,128)S(1)} %collective-permute-done.7.refs_1_), channel_id=1, source_target_pairs={{0,8},{1,9},{2,10},{3,11},{4,12},{5,13},{6,14},{7,15},{8,0},{9,1},... | collective-permute-start | bytes 786440 | tf_op jit(solution)/shard_map/ppermute | solution.py:31
  37.0 6.4 %collective-permute-start.11 = (f32[64,1024]{1,0:T(8,128)S(1)}, f32[64,1024]{1,0:T(8,128)S(1)}, u32[]{:S(2)}, u32[]{:S(2)}) collective-permute-start(f32[64,1024]{1,0:T(8,128)S(1)} %collective-permute-done.10.refs_5_), channel_id=1, source_target_pairs={{0,4},{1,3},{2,6},{3,1},{4,0},{5,7},{6,2},{7,5},{8,12},{9,11},{10,... | collective-permute-start | bytes 786440 | tf_op jit(solution)/shard_map/ppermute | solution.py:31

commit v4 on v3

--- a/solution.py
+++ b/solution.py
@@ -155,19 +155,20 @@
     own_d = send(own_a, second)
     near_a = send(near, first)
     far, own_b, high = together(far, own_b, high)
+    own_a, near, own_d = together(own_a, near, own_d)
     last = send(far, layer[1])
     far_a = send(far, first)
     own_a, far, own_d, own_b, near_a = together(own_a, far, own_d, own_b, near_a)
     far_b = send(far, second)
     near_b = send(own_b, layer[1])
+    total = subtract_round(static_flex, (own, own_a, near, own_b), high, low, 0)
     far_d = send(far_a, second)
     near_d = send(near_a, second)
-    total = subtract_round(static_flex, (own, own_a, near, own_b), high, low, 0)
-    last, total = together(last, total)
     last_a = send(last, first)
     last_b = send(far_b, layer[1])
+    last_a, total = together(last_a, total)
+    total = subtract_round(total, (far, own_d, near_a, last), high, low, 1)
     last_d = send(last_a, second)
-    total = subtract_round(total, (far, own_d, near_a, last), high, low, 1)
     total = subtract_round(total, (far_a, far_b, near_b, far_d, near_d, last_a), high, low, 2)
     return subtract_round(total, (last_b, last_d), high, low, 3)
 

time: 45.2 us -> 45.2 us (level)
  starting transfers between devices: 19.3 us -> 20 us
  waiting for transfers between devices: 16.9 us -> 16.2 us
    ppermute x15, waiting for transfers between devices: 16.8 us -> 16.2 us  [send(): return lax.ppermute(value, ('col', 'row'), pairs)]
    ppermute x15, starting transfers between devices: 18.9 us -> 19.5 us  [send(): return lax.ppermute(value, ('col', 'row'), pairs)]
  transfers between devices with their start and end apart: 16 -> 16, of which waited for: 7 -> 6; matrix products, arithmetic and copies ran while one was open for 3% -> 3% of each run, Pallas kernels for 10% -> 10%
where the time goes in v4:
time: 45.2 us; the launch traced here: 45 us
  starting transfers between devices  20 us (44%)
  waiting for transfers between devices  16.2 us (36%)
  Pallas kernels  6.33 us (14%)
  local copies, waits for them, and re-layouts  1.23 us (3%)
  other arithmetic  1.22 us (3%)
    ppermute x15, starting transfers between devices, send(): return lax.ppermute(value, ('col', 'row'), pairs)  19.5 us
    ppermute x15, waiting for transfers between devices, send(): return lax.ppermute(value, ('col', 'row'), pairs)  16.2 us
    pallas_call x4, Pallas kernels, subtract_round(): pl.pallas_call(functools.partial(last_kernel if last else round_kernel, m...  5.28 us
    unnamed x4, local copies, waits for them, and re-layouts  1.23 us
    div x1, other arithmetic, local_by_layers(): own = phi_slab.T / eigenvalues[:, None]  1.22 us
    pallas_call x1, Pallas kernels, prepare(): pl.pallas_call(functools.partial(prepare_kernel, order), out_shape=(shape...  1.05 us
  transfers between devices with their start and end apart: 16, of which 6 were waited for; matrix products, arithmetic and copies ran while one was open for 3% of the time, Pallas kernels for 10%

profile of v4, /device:TPU:0, one launch (start us, length us, event | category | flops | bytes accessed | tf_op | source)
XLA Modules:
  0.0 45.0 jit_solution(11585252063624123288)
XLA Ops:
  0.0 0.0 copy-start
  0.0 0.5 %collective-permute-start.5 = (f32[512,512]{1,0:T(8,128)}, f32[512,512]{1,0:T(8,128)S(1)}, u32[]{:S(2)}, u32[]{:S(2)}) collective-permute-start(f32[512,512]{1,0:T(8,128)} %mine_ref.1), channel_id=1, source_target_pairs={{0,1},{1,0},{2,3},{3,2},{4,5},{5,4},{6,7},{7,6},{8,9},{9,8},{10,11... | collective-permute-start | bytes 3145736 | tf_op jit(solution)/shard_map/ppermute | solution.py:148
  0.5 1.2 %divide_bitcast_fusion.refs_0_ = f32[64,1024]{1,0:T(8,128)S(1)} fusion(f32[1024,64]{0,1:T(8,128)} %param.5, f32[64]{0:T(128)} %param.7), kind=kLoop, calls=%fused_computation | loop fusion | flops 65536 | bytes 524544 | tf_op jit(solution)/shard_map/div | solution.py:149
  1.7 2.5 %collective-permute-start = (f32[64,1024]{1,0:T(8,128)S(1)}, f32[64,1024]{1,0:T(8,128)S(1)}, u32[]{:S(2)}, u32[]{:S(2)}) collective-permute-start(f32[64,1024]{1,0:T(8,128)S(1)} %divide_bitcast_fusion.refs_0_), channel_id=1, source_target_pairs={{0,2},{1,5},{2,0},{3,7},{4,6},{5,1},{6,4},{7,3},{8,10},{9,13},{10,... | collective-permute-start | bytes 786440 | tf_op jit(solution)/shard_map/ppermute | solution.py:31
  4.2 1.6 %collective-permute-start.1 = (f32[64,1024]{1,0:T(8,128)S(1)}, f32[64,1024]{1,0:T(8,128)S(1)}, u32[]{:S(2)}, u32[]{:S(2)}) collective-permute-start(f32[64,1024]{1,0:T(8,128)S(1)} %divide_bitcast_fusion.refs_0_), channel_id=1, source_target_pairs={{0,8},{1,9},{2,10},{3,11},{4,12},{5,13},{6,14},{7,15},{8,0},{9,1},... | collective-permute-start | bytes 786440 | tf_op jit(solution)/shard_map/ppermute | solution.py:31
  5.8 2.6 %collective-permute-start.3 = (f32[64,1024]{1,0:T(8,128)S(1)}, f32[64,1024]{1,0:T(8,128)S(1)}, u32[]{:S(2)}, u32[]{:S(2)}) collective-permute-start(f32[64,1024]{1,0:T(8,128)S(1)} %divide_bitcast_fusion.refs_0_), channel_id=1, source_target_pairs={{0,16},{1,17},{2,18},{3,19},{4,20},{5,21},{6,22},{7,23},{8,24},{9,... | collective-permute-start | bytes 786440 | tf_op jit(solution)/shard_map/ppermute | solution.py:31
  8.4 1.5 %collective-permute-start.4 = (f32[64,1024]{1,0:T(8,128)S(1)}, f32[64,1024]{1,0:T(8,128)S(1)}, u32[]{:S(2)}, u32[]{:S(2)}) collective-permute-start(f32[64,1024]{1,0:T(8,128)S(1)} %divide_bitcast_fusion.refs_0_), channel_id=1, source_target_pairs={{0,4},{1,3},{2,6},{3,1},{4,0},{5,7},{6,2},{7,5},{8,12},{9,11},{10,... | collective-permute-start | bytes 786440 | tf_op jit(solution)/shard_map/ppermute | solution.py:31
  9.9 0.0 collective-permute-done.refs_1_
  9.9 0.7 %collective-permute-start.2 = (f32[64,1024]{1,0:T(8,128)S(1)}, f32[64,1024]{1,0:T(8,128)S(1)}, u32[]{:S(2)}, u32[]{:S(2)}) collective-permute-start(f32[64,1024]{1,0:T(8,128)S(1)} %collective-permute-done.refs_1_), channel_id=1, source_target_pairs={{0,4},{1,3},{2,6},{3,1},{4,0},{5,7},{6,2},{7,5},{8,12},{9,11},{10,... | collective-permute-start | bytes 786440 | tf_op jit(solution)/shard_map/ppermute | solution.py:31
  10.6 7.4 %collective-permute-done.1.refs_2_ = f32[64,1024]{1,0:T(8,128)S(1)} collective-permute-done((f32[64,1024]{1,0:T(8,128)S(1)}, f32[64,1024]{1,0:T(8,128)S(1)}, u32[]{:S(2)}, u32[]{:S(2)}) %collective-permute-start.1) | collective-permute-done | bytes 262176 | tf_op jit(solution)/shard_map/ppermute | solution.py:31
  18.0 0.4 collective-permute-start.6
  18.4 0.0 collective-permute-done.5.other_ref
  18.4 0.0 copy-start.1
  18.4 1.2 %copy-done.1 = f32[512,512]{1,0:T(8,128)S(1)} copy-done((f32[512,512]{1,0:T(8,128)S(1)}, f32[512,512]{1,0:T(8,128)}, u32[]{:S(2)}) %copy-start.1) | copy-done | bytes 1048600
  19.6 1.1 %prepare_cols.1 = (bf16[1024,512]{1,0:T(8,128)(2,1)S(1)}, bf16[1024,512]{1,0:T(8,128)(2,1)S(1)}) custom-call(f32[512,512]{1,0:T(8,128)S(1)} %copy-done.1, f32[512,512]{1,0:T(8,128)S(1)} %collective-permute-done.5.other_ref), custom_call_target="tpu_custom_call" | custom-call | bytes 4194304 | tf_op jit(solution)/shard_map/prepare_cols/pallas_call | solution.py:81
  20.7 0.0 collective-permute-done.3.refs_0_
  20.7 0.0 collective-permute-done.4.refs_3_
  20.7 0.1 collective-permute-start.9
  20.8 1.7 %collective-permute-start.12 = (f32[64,1024]{1,0:T(8,128)S(1)}, f32[64,1024]{1,0:T(8,128)S(1)}, u32[]{:S(2)}, u32[]{:S(2)}) collective-permute-start(f32[64,1024]{1,0:T(8,128)S(1)} %collective-permute-done.3.refs_0_), channel_id=1, source_target_pairs={{0,2},{1,5},{2,0},{3,7},{4,6},{5,1},{6,4},{7,3},{8,10},{9,13},{10,... | collective-permute-start | bytes 786440 | tf_op jit(solution)/shard_map/ppermute | solution.py:31
  22.5 0.0 collective-permute-done.2.refs_1_
  22.5 1.9 %collective-permute-done.6.refs_2_ = f32[64,1024]{1,0:T(8,128)S(1)} collective-permute-done((f32[64,1024]{1,0:T(8,128)S(1)}, f32[64,1024]{1,0:T(8,128)S(1)}, u32[]{:S(2)}, u32[]{:S(2)}) %collective-permute-start.6) | collective-permute-done | bytes 262176 | tf_op jit(solution)/shard_map/ppermute | solution.py:31
  24.4 0.4 collective-permute-start.7
  24.8 3.1 %collective-permute-done.9.refs_3_ = f32[64,1024]{1,0:T(8,128)S(1)} collective-permute-done((f32[64,1024]{1,0:T(8,128)S(1)}, f32[64,1024]{1,0:T(8,128)S(1)}, u32[]{:S(2)}, u32[]{:S(2)}) %collective-permute-start.9) | collective-permute-done | bytes 262176 | tf_op jit(solution)/shard_map/ppermute | solution.py:31
  27.9 2.1 %collective-permute-start.10 = (f32[64,1024]{1,0:T(8,128)S(1)}, f32[64,1024]{1,0:T(8,128)S(1)}, u32[]{:S(2)}, u32[]{:S(2)}) collective-permute-start(f32[64,1024]{1,0:T(8,128)S(1)} %collective-permute-done.9.refs_3_), channel_id=1, source_target_pairs={{0,2},{1,5},{2,0},{3,7},{4,6},{5,1},{6,4},{7,3},{8,10},{9,13},{10,... | collective-permute-start | bytes 786440 | tf_op jit(solution)/shard_map/ppermute | solution.py:31
  30.0 0.4 collective-permute-start.13
  30.4 1.2 %collective-permute-start.15 = (f32[64,1024]{1,0:T(8,128)S(1)}, f32[64,1024]{1,0:T(8,128)S(1)}, u32[]{:S(2)}, u32[]{:S(2)}) collective-permute-start(f32[64,1024]{1,0:T(8,128)S(1)} %collective-permute-done.6.refs_2_), channel_id=1, source_target_pairs={{0,4},{1,3},{2,6},{3,1},{4,0},{5,7},{6,2},{7,5},{8,12},{9,11},{10,... | collective-permute-start | bytes 786440 | tf_op jit(solution)/shard_map/ppermute | solution.py:31
  31.6 0.0 collective-permute-done.12.refs_0_
  31.6 0.8 %collective-permute-start.14 = (f32[64,1024]{1,0:T(8,128)S(1)}, f32[64,1024]{1,0:T(8,128)S(1)}, u32[]{:S(2)}, u32[]{:S(2)}) collective-permute-start(f32[64,1024]{1,0:T(8,128)S(1)} %collective-permute-done.12.refs_0_), channel_id=1, source_target_pairs={{0,4},{1,3},{2,6},{3,1},{4,0},{5,7},{6,2},{7,5},{8,12},{9,11},{10,... | collective-permute-start | bytes 786440 | tf_op jit(solution)/shard_map/ppermute | solution.py:31
  32.4 0.0 copy-done
  32.4 1.0 %subtract_round.3.refs_6_ = f32[1024,512]{1,0:T(8,128)S(1)} custom-call(f32[64,1024]{1,0:T(8,128)S(1)} %divide_bitcast_fusion.refs_0_, f32[64,1024]{1,0:T(8,128)S(1)} %collective-permute-done.refs_1_, f32[64,1024]{1,0:T(8,128)S(1)} %collective-permute-done.1.refs_2_, f32[64,1024]{1,0:T(8,128)S(1)} %collective-permute-done.4.refs_3_, ...), custom_call_target="tpu_custom_call" | custom-call | flops 805306368 | bytes 4194304 | tf_op jit(solution)/shard_map/subtract_round/pallas_call | solution.py:134
  33.5 0.0 collective-permute-done.7.refs_1_
  33.5 1.7 %collective-permute-start.8 = (f32[64,1024]{1,0:T(8,128)S(1)}, f32[64,1024]{1,0:T(8,128)S(1)}, u32[]{:S(2)}, u32[]{:S(2)}) collective-permute-start(f32[64,1024]{1,0:T(8,128)S(1)} %collective-permute-done.7.refs_1_), channel_id=1, source_target_pairs={{0,8},{1,9},{2,10},{3,11},{4,12},{5,13},{6,14},{7,15},{8,0},{9,1},... | collective-permute-start | bytes 786440 | tf_op jit(solution)/shard_map/ppermute | solution.py:31
  35.2 1.8 %collective-permute-done.10.refs_5_ = f32[64,1024]{1,0:T(8,128)S(1)} collective-permute-done((f32[64,1024]{1,0:T(8,128)S(1)}, f32[64,1024]{1,0:T(8,128)S(1)}, u32[]{:S(2)}, u32[]{:S(2)}) %collective-permute-start.10) | collective-permute-done | bytes 262176 | tf_op jit(solution)/shard_map/ppermute | solution.py:31
  37.0 1.8 %collective-permute-start.11 = (f32[64,1024]{1,0:T(8,128)S(1)}, f32[64,1024]{1,0:T(8,128)S(1)}, u32[]{:S(2)}, u32[]{:S(2)}) collective-permute-start(f32[64,1024]{1,0:T(8,128)S(1)} %collective-permute-done.10.refs_5_), channel_id=1, source_target_pairs={{0,4},{1,3},{2,6},{3,1},{4,0},{5,7},{6,2},{7,5},{8,12},{9,11},{10,... | collective-permute-start | bytes 786440 | tf_op jit(solution)/shard_map/ppermute | solution.py:31
  38.8 1.0 %subtract_round.4.refs_8_ = f32[1024,512]{1,0:T(8,128)S(1)} custom-call(f32[64,1024]{1,0:T(8,128)S(1)} %collective-permute-done.3.refs_0_, f32[64,1024]{1,0:T(8,128)S(1)} %collective-permute-done.2.refs_1_, f32[64,1024]{1,0:T(8,128)S(1)} %collective-permute-done.6.refs_2_, f32[64,1024]{1,0:T(8,128)S(1)} %collective-permute-done.9.refs_3_, ...), custom_call_target="tpu_custom_call" | custom-call | flops 805306368 | bytes 4194304 | tf_op jit(solution)/shard_map/subtract_round/pallas_call | solution.py:134
  39.9 0.0 collective-permute-done.13.refs_2_
  39.9 0.0 collective-permute-done.15.refs_4_
  39.9 0.0 collective-permute-done.14.refs_3_
  39.9 1.6 %subtract_round.5.refs_4_ = f32[1024,512]{1,0:T(8,128)S(1)} custom-call(f32[64,1024]{1,0:T(8,128)S(1)} %collective-permute-done.12.refs_0_, f32[64,1024]{1,0:T(8,128)S(1)} %collective-permute-done.7.refs_1_, f32[64,1024]{1,0:T(8,128)S(1)} %collective-permute-done.13.refs_2_, f32[64,1024]{1,0:T(8,128)S(1)} %collective-permute-done.14.refs_3_, ...), custom_call_target="tpu_custom_call" | custom-call | flops 1207959552 | bytes 4194304 | tf_op jit(solution)/shard_map/subtract_round/pallas_call | solution.py:134
  41.5 0.5 %collective-permute-done.8.refs_0_ = f32[64,1024]{1,0:T(8,128)S(1)} collective-permute-done((f32[64,1024]{1,0:T(8,128)S(1)}, f32[64,1024]{1,0:T(8,128)S(1)}, u32[]{:S(2)}, u32[]{:S(2)}) %collective-permute-start.8) | collective-permute-done | bytes 262176 | tf_op jit(solution)/shard_map/ppermute | solution.py:31
  42.0 1.4 %collective-permute-done.11.refs_1_ = f32[64,1024]{1,0:T(8,128)S(1)} collective-permute-done((f32[64,1024]{1,0:T(8,128)S(1)}, f32[64,1024]{1,0:T(8,128)S(1)}, u32[]{:S(2)}, u32[]{:S(2)}) %collective-permute-start.11) | collective-permute-done | bytes 262176 | tf_op jit(solution)/shard_map/ppermute | solution.py:31
  43.4 1.6 %subtract_last.1 = f32[1024,512]{1,0:T(8,128)} custom-call(f32[64,1024]{1,0:T(8,128)S(1)} %collective-permute-done.8.refs_0_, f32[64,1024]{1,0:T(8,128)S(1)} %collective-permute-done.11.refs_1_, bf16[1024,512]{1,0:T(8,128)(2,1)S(1)} %get-tuple-element.29.refs_4_.refs_6_.refs_2_, bf16[1024,512]{1,0:T(8,128)(2,1)S(1)} %get-tuple-element.30.refs_5_.refs_7_.refs_3_, ...), custom_call_target="tpu_custom_call" | custom-call | flops 402653184 | bytes 4194304 | tf_op jit(solution)/shard_map/subtract_last/pallas_call | solution.py:134
Async XLA Ops:
  0.0 32.4 %copy-start = (f32[1024,512]{1,0:T(8,128)S(1)}, f32[1024,512]{1,0:T(8,128)}, u32[]{:S(2)}) copy-start(f32[1024,512]{1,0:T(8,128)} %refs_6_.1) | copy-start | bytes 6291460
  0.0 18.4 %collective-permute-start.5 = (f32[512,512]{1,0:T(8,128)}, f32[512,512]{1,0:T(8,128)S(1)}, u32[]{:S(2)}, u32[]{:S(2)}) collective-permute-start(f32[512,512]{1,0:T(8,128)} %mine_ref.1), channel_id=1, source_target_pairs={{0,1},{1,0},{2,3},{3,2},{4,5},{5,4},{6,7},{7,6},{8,9},{9,8},{10,11... | collective-permute-start | bytes 3145736 | tf_op jit(solution)/shard_map/ppermute | solution.py:148
  1.7 8.2 %collective-permute-start = (f32[64,1024]{1,0:T(8,128)S(1)}, f32[64,1024]{1,0:T(8,128)S(1)}, u32[]{:S(2)}, u32[]{:S(2)}) collective-permute-start(f32[64,1024]{1,0:T(8,128)S(1)} %divide_bitcast_fusion.refs_0_), channel_id=1, source_target_pairs={{0,2},{1,5},{2,0},{3,7},{4,6},{5,1},{6,4},{7,3},{8,10},{9,13},{10,... | collective-permute-start | bytes 786440 | tf_op jit(solution)/shard_map/ppermute | solution.py:31
  4.2 13.8 %collective-permute-start.1 = (f32[64,1024]{1,0:T(8,128)S(1)}, f32[64,1024]{1,0:T(8,128)S(1)}, u32[]{:S(2)}, u32[]{:S(2)}) collective-permute-start(f32[64,1024]{1,0:T(8,128)S(1)} %divide_bitcast_fusion.refs_0_), channel_id=1, source_target_pairs={{0,8},{1,9},{2,10},{3,11},{4,12},{5,13},{6,14},{7,15},{8,0},{9,1},... | collective-permute-start | bytes 786440 | tf_op jit(solution)/shard_map/ppermute | solution.py:31
  5.8 14.9 %collective-permute-start.3 = (f32[64,1024]{1,0:T(8,128)S(1)}, f32[64,1024]{1,0:T(8,128)S(1)}, u32[]{:S(2)}, u32[]{:S(2)}) collective-permute-start(f32[64,1024]{1,0:T(8,128)S(1)} %divide_bitcast_fusion.refs_0_), channel_id=1, source_target_pairs={{0,16},{1,17},{2,18},{3,19},{4,20},{5,21},{6,22},{7,23},{8,24},{9,... | collective-permute-start | bytes 786440 | tf_op jit(solution)/shard_map/ppermute | solution.py:31
  8.4 12.3 %collective-permute-start.4 = (f32[64,1024]{1,0:T(8,128)S(1)}, f32[64,1024]{1,0:T(8,128)S(1)}, u32[]{:S(2)}, u32[]{:S(2)}) collective-permute-start(f32[64,1024]{1,0:T(8,128)S(1)} %divide_bitcast_fusion.refs_0_), channel_id=1, source_target_pairs={{0,4},{1,3},{2,6},{3,1},{4,0},{5,7},{6,2},{7,5},{8,12},{9,11},{10,... | collective-permute-start | bytes 786440 | tf_op jit(solution)/shard_map/ppermute | solution.py:31
  9.9 12.6 %collective-permute-start.2 = (f32[64,1024]{1,0:T(8,128)S(1)}, f32[64,1024]{1,0:T(8,128)S(1)}, u32[]{:S(2)}, u32[]{:S(2)}) collective-permute-start(f32[64,1024]{1,0:T(8,128)S(1)} %collective-permute-done.refs_1_), channel_id=1, source_target_pairs={{0,4},{1,3},{2,6},{3,1},{4,0},{5,7},{6,2},{7,5},{8,12},{9,11},{10,... | collective-permute-start | bytes 786440 | tf_op jit(solution)/shard_map/ppermute | solution.py:31
  18.0 6.4 %collective-permute-start.6 = (f32[64,1024]{1,0:T(8,128)S(1)}, f32[64,1024]{1,0:T(8,128)S(1)}, u32[]{:S(2)}, u32[]{:S(2)}) collective-permute-start(f32[64,1024]{1,0:T(8,128)S(1)} %collective-permute-done.1.refs_2_), channel_id=1, source_target_pairs={{0,2},{1,5},{2,0},{3,7},{4,6},{5,1},{6,4},{7,3},{8,10},{9,13},{10,... | collective-permute-start | bytes 786440 | tf_op jit(solution)/shard_map/ppermute | solution.py:31
  18.4 1.2 %copy-start.1 = (f32[512,512]{1,0:T(8,128)S(1)}, f32[512,512]{1,0:T(8,128)}, u32[]{:S(2)}) copy-start(f32[512,512]{1,0:T(8,128)} %mine_ref.1) | copy-start | bytes 3145732
  20.7 7.2 %collective-permute-start.9 = (f32[64,1024]{1,0:T(8,128)S(1)}, f32[64,1024]{1,0:T(8,128)S(1)}, u32[]{:S(2)}, u32[]{:S(2)}) collective-permute-start(f32[64,1024]{1,0:T(8,128)S(1)} %collective-permute-done.3.refs_0_), channel_id=1, source_target_pairs={{0,8},{1,9},{2,10},{3,11},{4,12},{5,13},{6,14},{7,15},{8,0},{9,1},... | collective-permute-start | bytes 786440 | tf_op jit(solution)/shard_map/ppermute | solution.py:31
  20.8 10.8 %collective-permute-start.12 = (f32[64,1024]{1,0:T(8,128)S(1)}, f32[64,1024]{1,0:T(8,128)S(1)}, u32[]{:S(2)}, u32[]{:S(2)}) collective-permute-start(f32[64,1024]{1,0:T(8,128)S(1)} %collective-permute-done.3.refs_0_), channel_id=1, source_target_pairs={{0,2},{1,5},{2,0},{3,7},{4,6},{5,1},{6,4},{7,3},{8,10},{9,13},{10,... | collective-permute-start | bytes 786440 | tf_op jit(solution)/shard_map/ppermute | solution.py:31
  24.4 9.1 %collective-permute-start.7 = (f32[64,1024]{1,0:T(8,128)S(1)}, f32[64,1024]{1,0:T(8,128)S(1)}, u32[]{:S(2)}, u32[]{:S(2)}) collective-permute-start(f32[64,1024]{1,0:T(8,128)S(1)} %collective-permute-done.3.refs_0_), channel_id=1, source_target_pairs={{0,4},{1,3},{2,6},{3,1},{4,0},{5,7},{6,2},{7,5},{8,12},{9,11},{10,... | collective-permute-start | bytes 786440 | tf_op jit(solution)/shard_map/ppermute | solution.py:31
  27.9 9.1 %collective-permute-start.10 = (f32[64,1024]{1,0:T(8,128)S(1)}, f32[64,1024]{1,0:T(8,128)S(1)}, u32[]{:S(2)}, u32[]{:S(2)}) collective-permute-start(f32[64,1024]{1,0:T(8,128)S(1)} %collective-permute-done.9.refs_3_), channel_id=1, source_target_pairs={{0,2},{1,5},{2,0},{3,7},{4,6},{5,1},{6,4},{7,3},{8,10},{9,13},{10,... | collective-permute-start | bytes 786440 | tf_op jit(solution)/shard_map/ppermute | solution.py:31
  30.0 9.9 %collective-permute-start.13 = (f32[64,1024]{1,0:T(8,128)S(1)}, f32[64,1024]{1,0:T(8,128)S(1)}, u32[]{:S(2)}, u32[]{:S(2)}) collective-permute-start(f32[64,1024]{1,0:T(8,128)S(1)} %collective-permute-done.4.refs_3_), channel_id=1, source_target_pairs={{0,8},{1,9},{2,10},{3,11},{4,12},{5,13},{6,14},{7,15},{8,0},{9,1},... | collective-permute-start | bytes 786440 | tf_op jit(solution)/shard_map/ppermute | solution.py:31
  30.4 9.5 %collective-permute-start.15 = (f32[64,1024]{1,0:T(8,128)S(1)}, f32[64,1024]{1,0:T(8,128)S(1)}, u32[]{:S(2)}, u32[]{:S(2)}) collective-permute-start(f32[64,1024]{1,0:T(8,128)S(1)} %collective-permute-done.6.refs_2_), channel_id=1, source_target_pairs={{0,4},{1,3},{2,6},{3,1},{4,0},{5,7},{6,2},{7,5},{8,12},{9,11},{10,... | collective-permute-start | bytes 786440 | tf_op jit(solution)/shard_map/ppermute | solution.py:31
  31.6 8.3 %collective-permute-start.14 = (f32[64,1024]{1,0:T(8,128)S(1)}, f32[64,1024]{1,0:T(8,128)S(1)}, u32[]{:S(2)}, u32[]{:S(2)}) collective-permute-start(f32[64,1024]{1,0:T(8,128)S(1)} %collective-permute-done.12.refs_0_), channel_id=1, source_target_pairs={{0,4},{1,3},{2,6},{3,1},{4,0},{5,7},{6,2},{7,5},{8,12},{9,11},{10,... | collective-permute-start | bytes 786440 | tf_op jit(solution)/shard_map/ppermute | solution.py:31
  33.5 8.5 %collective-permute-start.8 = (f32[64,1024]{1,0:T(8,128)S(1)}, f32[64,1024]{1,0:T(8,128)S(1)}, u32[]{:S(2)}, u32[]{:S(2)}) collective-permute-start(f32[64,1024]{1,0:T(8,128)S(1)} %collective-permute-done.7.refs_1_), channel_id=1, source_target_pairs={{0,8},{1,9},{2,10},{3,11},{4,12},{5,13},{6,14},{7,15},{8,0},{9,1},... | collective-permute-start | bytes 786440 | tf_op jit(solution)/shard_map/ppermute | solution.py:31
  37.0 6.4 %collective-permute-start.11 = (f32[64,1024]{1,0:T(8,128)S(1)}, f32[64,1024]{1,0:T(8,128)S(1)}, u32[]{:S(2)}, u32[]{:S(2)}) collective-permute-start(f32[64,1024]{1,0:T(8,128)S(1)} %collective-permute-done.10.refs_5_), channel_id=1, source_target_pairs={{0,4},{1,3},{2,6},{3,1},{4,0},{5,7},{6,2},{7,5},{8,12},{9,11},{10,... | collective-permute-start | bytes 786440 | tf_op jit(solution)/shard_map/ppermute | solution.py:31

commit v5 on v4

--- a/solution.py
+++ b/solution.py
@@ -37,8 +37,8 @@
 
 ROUNDS = (
     ((0, 0), (0, 1), (1, 0), (0, 2)),
-    ((2, 0), (0, 3), (1, 1), (3, 0)),
-    ((2, 1), (2, 2), (1, 2), (2, 3), (1, 3), (3, 1)),
+    ((2, 0), (0, 3), (1, 1), (3, 0), (2, 1), (2, 2)),
+    ((1, 2), (2, 3), (1, 3), (3, 1)),
     ((3, 2), (3, 3)),
 )
 
@@ -167,9 +167,9 @@
     last_a = send(last, first)
     last_b = send(far_b, layer[1])
     last_a, total = together(last_a, total)
-    total = subtract_round(total, (far, own_d, near_a, last), high, low, 1)
+    total = subtract_round(total, (far, own_d, near_a, last, far_a, far_b), high, low, 1)
     last_d = send(last_a, second)
-    total = subtract_round(total, (far_a, far_b, near_b, far_d, near_d, last_a), high, low, 2)
+    total = subtract_round(total, (near_b, far_d, near_d, last_a), high, low, 2)
     return subtract_round(total, (last_b, last_d), high, low, 3)
 
 

time: 45.2 us -> 45.2 us (level)
  no operation moved by 1% of the time
where the time goes in v5:
time: 45.2 us; the launch traced here: 45 us
  starting transfers between devices  20 us (44%)
  waiting for transfers between devices  16.2 us (36%)
  Pallas kernels  6.33 us (14%)
  local copies, waits for them, and re-layouts  1.23 us (3%)
  other arithmetic  1.22 us (3%)
    ppermute x15, starting transfers between devices, send(): return lax.ppermute(value, ('col', 'row'), pairs)  19.5 us
    ppermute x15, waiting for transfers between devices, send(): return lax.ppermute(value, ('col', 'row'), pairs)  16.2 us
    pallas_call x4, Pallas kernels, subtract_round(): pl.pallas_call(functools.partial(last_kernel if last else round_kernel, m...  5.27 us
    unnamed x4, local copies, waits for them, and re-layouts  1.23 us
    div x1, other arithmetic, local_by_layers(): own = phi_slab.T / eigenvalues[:, None]  1.22 us
    pallas_call x1, Pallas kernels, prepare(): pl.pallas_call(functools.partial(prepare_kernel, order), out_shape=(shape...  1.05 us
  transfers between devices with their start and end apart: 16, of which 6 were waited for; matrix products, arithmetic and copies ran while one was open for 3% of the time, Pallas kernels for 10%

profile of v5, /device:TPU:0, one launch (start us, length us, event | category | flops | bytes accessed | tf_op | source)
XLA Modules:
  0.0 45.0 jit_solution(18213647861397452658)
XLA Ops:
  0.0 0.0 copy-start
  0.0 0.5 %collective-permute-start.5 = (f32[512,512]{1,0:T(8,128)}, f32[512,512]{1,0:T(8,128)S(1)}, u32[]{:S(2)}, u32[]{:S(2)}) collective-permute-start(f32[512,512]{1,0:T(8,128)} %mine_ref.1), channel_id=1, source_target_pairs={{0,1},{1,0},{2,3},{3,2},{4,5},{5,4},{6,7},{7,6},{8,9},{9,8},{10,11... | collective-permute-start | bytes 3145736 | tf_op jit(solution)/shard_map/ppermute | solution.py:148
  0.5 1.2 %divide_bitcast_fusion.refs_0_ = f32[64,1024]{1,0:T(8,128)S(1)} fusion(f32[1024,64]{0,1:T(8,128)} %param.5, f32[64]{0:T(128)} %param.7), kind=kLoop, calls=%fused_computation | loop fusion | flops 65536 | bytes 524544 | tf_op jit(solution)/shard_map/div | solution.py:149
  1.7 2.5 %collective-permute-start = (f32[64,1024]{1,0:T(8,128)S(1)}, f32[64,1024]{1,0:T(8,128)S(1)}, u32[]{:S(2)}, u32[]{:S(2)}) collective-permute-start(f32[64,1024]{1,0:T(8,128)S(1)} %divide_bitcast_fusion.refs_0_), channel_id=1, source_target_pairs={{0,2},{1,5},{2,0},{3,7},{4,6},{5,1},{6,4},{7,3},{8,10},{9,13},{10,... | collective-permute-start | bytes 786440 | tf_op jit(solution)/shard_map/ppermute | solution.py:31
  4.2 1.6 %collective-permute-start.1 = (f32[64,1024]{1,0:T(8,128)S(1)}, f32[64,1024]{1,0:T(8,128)S(1)}, u32[]{:S(2)}, u32[]{:S(2)}) collective-permute-start(f32[64,1024]{1,0:T(8,128)S(1)} %divide_bitcast_fusion.refs_0_), channel_id=1, source_target_pairs={{0,8},{1,9},{2,10},{3,11},{4,12},{5,13},{6,14},{7,15},{8,0},{9,1},... | collective-permute-start | bytes 786440 | tf_op jit(solution)/shard_map/ppermute | solution.py:31
  5.8 2.6 %collective-permute-start.3 = (f32[64,1024]{1,0:T(8,128)S(1)}, f32[64,1024]{1,0:T(8,128)S(1)}, u32[]{:S(2)}, u32[]{:S(2)}) collective-permute-start(f32[64,1024]{1,0:T(8,128)S(1)} %divide_bitcast_fusion.refs_0_), channel_id=1, source_target_pairs={{0,16},{1,17},{2,18},{3,19},{4,20},{5,21},{6,22},{7,23},{8,24},{9,... | collective-permute-start | bytes 786440 | tf_op jit(solution)/shard_map/ppermute | solution.py:31
  8.4 1.5 %collective-permute-start.4 = (f32[64,1024]{1,0:T(8,128)S(1)}, f32[64,1024]{1,0:T(8,128)S(1)}, u32[]{:S(2)}, u32[]{:S(2)}) collective-permute-start(f32[64,1024]{1,0:T(8,128)S(1)} %divide_bitcast_fusion.refs_0_), channel_id=1, source_target_pairs={{0,4},{1,3},{2,6},{3,1},{4,0},{5,7},{6,2},{7,5},{8,12},{9,11},{10,... | collective-permute-start | bytes 786440 | tf_op jit(solution)/shard_map/ppermute | solution.py:31
  9.9 0.0 collective-permute-done.refs_1_
  9.9 0.7 %collective-permute-start.2 = (f32[64,1024]{1,0:T(8,128)S(1)}, f32[64,1024]{1,0:T(8,128)S(1)}, u32[]{:S(2)}, u32[]{:S(2)}) collective-permute-start(f32[64,1024]{1,0:T(8,128)S(1)} %collective-permute-done.refs_1_), channel_id=1, source_target_pairs={{0,4},{1,3},{2,6},{3,1},{4,0},{5,7},{6,2},{7,5},{8,12},{9,11},{10,... | collective-permute-start | bytes 786440 | tf_op jit(solution)/shard_map/ppermute | solution.py:31
  10.6 7.4 %collective-permute-done.1.refs_2_ = f32[64,1024]{1,0:T(8,128)S(1)} collective-permute-done((f32[64,1024]{1,0:T(8,128)S(1)}, f32[64,1024]{1,0:T(8,128)S(1)}, u32[]{:S(2)}, u32[]{:S(2)}) %collective-permute-start.1) | collective-permute-done | bytes 262176 | tf_op jit(solution)/shard_map/ppermute | solution.py:31
  18.0 0.4 collective-permute-start.6
  18.4 0.0 collective-permute-done.5.other_ref
  18.4 0.0 copy-start.1
  18.4 1.2 %copy-done.1 = f32[512,512]{1,0:T(8,128)S(1)} copy-done((f32[512,512]{1,0:T(8,128)S(1)}, f32[512,512]{1,0:T(8,128)}, u32[]{:S(2)}) %copy-start.1) | copy-done | bytes 1048600
  19.6 1.1 %prepare_cols.1 = (bf16[1024,512]{1,0:T(8,128)(2,1)S(1)}, bf16[1024,512]{1,0:T(8,128)(2,1)S(1)}) custom-call(f32[512,512]{1,0:T(8,128)S(1)} %copy-done.1, f32[512,512]{1,0:T(8,128)S(1)} %collective-permute-done.5.other_ref), custom_call_target="tpu_custom_call" | custom-call | bytes 4194304 | tf_op jit(solution)/shard_map/prepare_cols/pallas_call | solution.py:81
  20.7 0.0 collective-permute-done.3.refs_0_
  20.7 0.0 collective-permute-done.4.refs_3_
  20.7 0.1 collective-permute-start.9
  20.8 1.7 %collective-permute-start.13 = (f32[64,1024]{1,0:T(8,128)S(1)}, f32[64,1024]{1,0:T(8,128)S(1)}, u32[]{:S(2)}, u32[]{:S(2)}) collective-permute-start(f32[64,1024]{1,0:T(8,128)S(1)} %collective-permute-done.3.refs_0_), channel_id=1, source_target_pairs={{0,2},{1,5},{2,0},{3,7},{4,6},{5,1},{6,4},{7,3},{8,10},{9,13},{10,... | collective-permute-start | bytes 786440 | tf_op jit(solution)/shard_map/ppermute | solution.py:31
  22.5 0.0 collective-permute-done.2.refs_1_
  22.5 1.9 %collective-permute-done.6.refs_2_ = f32[64,1024]{1,0:T(8,128)S(1)} collective-permute-done((f32[64,1024]{1,0:T(8,128)S(1)}, f32[64,1024]{1,0:T(8,128)S(1)}, u32[]{:S(2)}, u32[]{:S(2)}) %collective-permute-start.6) | collective-permute-done | bytes 262176 | tf_op jit(solution)/shard_map/ppermute | solution.py:31
  24.4 0.4 collective-permute-start.7
  24.8 3.1 %collective-permute-done.9.refs_3_ = f32[64,1024]{1,0:T(8,128)S(1)} collective-permute-done((f32[64,1024]{1,0:T(8,128)S(1)}, f32[64,1024]{1,0:T(8,128)S(1)}, u32[]{:S(2)}, u32[]{:S(2)}) %collective-permute-start.9) | collective-permute-done | bytes 262176 | tf_op jit(solution)/shard_map/ppermute | solution.py:31
  27.9 2.1 %collective-permute-start.10 = (f32[64,1024]{1,0:T(8,128)S(1)}, f32[64,1024]{1,0:T(8,128)S(1)}, u32[]{:S(2)}, u32[]{:S(2)}) collective-permute-start(f32[64,1024]{1,0:T(8,128)S(1)} %collective-permute-done.9.refs_3_), channel_id=1, source_target_pairs={{0,2},{1,5},{2,0},{3,7},{4,6},{5,1},{6,4},{7,3},{8,10},{9,13},{10,... | collective-permute-start | bytes 786440 | tf_op jit(solution)/shard_map/ppermute | solution.py:31
  30.0 0.4 collective-permute-start.12
  30.4 1.2 %collective-permute-start.15 = (f32[64,1024]{1,0:T(8,128)S(1)}, f32[64,1024]{1,0:T(8,128)S(1)}, u32[]{:S(2)}, u32[]{:S(2)}) collective-permute-start(f32[64,1024]{1,0:T(8,128)S(1)} %collective-permute-done.6.refs_2_), channel_id=1, source_target_pairs={{0,4},{1,3},{2,6},{3,1},{4,0},{5,7},{6,2},{7,5},{8,12},{9,11},{10,... | collective-permute-start | bytes 786440 | tf_op jit(solution)/shard_map/ppermute | solution.py:31
  31.6 0.0 collective-permute-done.13.refs_4_
  31.6 0.8 %collective-permute-start.14 = (f32[64,1024]{1,0:T(8,128)S(1)}, f32[64,1024]{1,0:T(8,128)S(1)}, u32[]{:S(2)}, u32[]{:S(2)}) collective-permute-start(f32[64,1024]{1,0:T(8,128)S(1)} %collective-permute-done.13.refs_4_), channel_id=1, source_target_pairs={{0,4},{1,3},{2,6},{3,1},{4,0},{5,7},{6,2},{7,5},{8,12},{9,11},{10,... | collective-permute-start | bytes 786440 | tf_op jit(solution)/shard_map/ppermute | solution.py:31
  32.4 0.0 copy-done
  32.4 1.0 %subtract_round.3.refs_8_ = f32[1024,512]{1,0:T(8,128)S(1)} custom-call(f32[64,1024]{1,0:T(8,128)S(1)} %divide_bitcast_fusion.refs_0_, f32[64,1024]{1,0:T(8,128)S(1)} %collective-permute-done.refs_1_, f32[64,1024]{1,0:T(8,128)S(1)} %collective-permute-done.1.refs_2_, f32[64,1024]{1,0:T(8,128)S(1)} %collective-permute-done.4.refs_3_, ...), custom_call_target="tpu_custom_call" | custom-call | flops 805306368 | bytes 4194304 | tf_op jit(solution)/shard_map/subtract_round/pallas_call | solution.py:134
  33.5 0.0 collective-permute-done.7.refs_5_
  33.5 1.7 %collective-permute-start.8 = (f32[64,1024]{1,0:T(8,128)S(1)}, f32[64,1024]{1,0:T(8,128)S(1)}, u32[]{:S(2)}, u32[]{:S(2)}) collective-permute-start(f32[64,1024]{1,0:T(8,128)S(1)} %collective-permute-done.7.refs_5_), channel_id=1, source_target_pairs={{0,8},{1,9},{2,10},{3,11},{4,12},{5,13},{6,14},{7,15},{8,0},{9,1},... | collective-permute-start | bytes 786440 | tf_op jit(solution)/shard_map/ppermute | solution.py:31
  35.2 1.8 %collective-permute-done.10.refs_3_ = f32[64,1024]{1,0:T(8,128)S(1)} collective-permute-done((f32[64,1024]{1,0:T(8,128)S(1)}, f32[64,1024]{1,0:T(8,128)S(1)}, u32[]{:S(2)}, u32[]{:S(2)}) %collective-permute-start.10) | collective-permute-done | bytes 262176 | tf_op jit(solution)/shard_map/ppermute | solution.py:31
  37.0 1.8 %collective-permute-start.11 = (f32[64,1024]{1,0:T(8,128)S(1)}, f32[64,1024]{1,0:T(8,128)S(1)}, u32[]{:S(2)}, u32[]{:S(2)}) collective-permute-start(f32[64,1024]{1,0:T(8,128)S(1)} %collective-permute-done.10.refs_3_), channel_id=1, source_target_pairs={{0,4},{1,3},{2,6},{3,1},{4,0},{5,7},{6,2},{7,5},{8,12},{9,11},{10,... | collective-permute-start | bytes 786440 | tf_op jit(solution)/shard_map/ppermute | solution.py:31
  38.8 1.6 %subtract_round.4.refs_6_ = f32[1024,512]{1,0:T(8,128)S(1)} custom-call(f32[64,1024]{1,0:T(8,128)S(1)} %collective-permute-done.3.refs_0_, f32[64,1024]{1,0:T(8,128)S(1)} %collective-permute-done.2.refs_1_, f32[64,1024]{1,0:T(8,128)S(1)} %collective-permute-done.6.refs_2_, f32[64,1024]{1,0:T(8,128)S(1)} %collective-permute-done.9.refs_3_, ...), custom_call_target="tpu_custom_call" | custom-call | flops 1207959552 | bytes 4194304 | tf_op jit(solution)/shard_map/subtract_round/pallas_call | solution.py:134
  40.4 0.0 collective-permute-done.12.refs_0_
  40.4 0.0 collective-permute-done.15.refs_2_
  40.4 0.0 collective-permute-done.14.refs_1_
  40.4 1.0 %subtract_round.5.refs_4_ = f32[1024,512]{1,0:T(8,128)S(1)} custom-call(f32[64,1024]{1,0:T(8,128)S(1)} %collective-permute-done.12.refs_0_, f32[64,1024]{1,0:T(8,128)S(1)} %collective-permute-done.14.refs_1_, f32[64,1024]{1,0:T(8,128)S(1)} %collective-permute-done.15.refs_2_, f32[64,1024]{1,0:T(8,128)S(1)} %collective-permute-done.10.refs_3_, ...), custom_call_target="tpu_custom_call" | custom-call | flops 805306368 | bytes 4194304 | tf_op jit(solution)/shard_map/subtract_round/pallas_call | solution.py:134
  41.5 0.5 %collective-permute-done.8.refs_0_ = f32[64,1024]{1,0:T(8,128)S(1)} collective-permute-done((f32[64,1024]{1,0:T(8,128)S(1)}, f32[64,1024]{1,0:T(8,128)S(1)}, u32[]{:S(2)}, u32[]{:S(2)}) %collective-permute-start.8) | collective-permute-done | bytes 262176 | tf_op jit(solution)/shard_map/ppermute | solution.py:31
  42.0 1.4 %collective-permute-done.11.refs_1_ = f32[64,1024]{1,0:T(8,128)S(1)} collective-permute-done((f32[64,1024]{1,0:T(8,128)S(1)}, f32[64,1024]{1,0:T(8,128)S(1)}, u32[]{:S(2)}, u32[]{:S(2)}) %collective-permute-start.11) | collective-permute-done | bytes 262176 | tf_op jit(solution)/shard_map/ppermute | solution.py:31
  43.4 1.6 %subtract_last.1 = f32[1024,512]{1,0:T(8,128)} custom-call(f32[64,1024]{1,0:T(8,128)S(1)} %collective-permute-done.8.refs_0_, f32[64,1024]{1,0:T(8,128)S(1)} %collective-permute-done.11.refs_1_, bf16[1024,512]{1,0:T(8,128)(2,1)S(1)} %get-tuple-element.29.refs_4_.refs_6_.refs_2_, bf16[1024,512]{1,0:T(8,128)(2,1)S(1)} %get-tuple-element.30.refs_5_.refs_7_.refs_3_, ...), custom_call_target="tpu_custom_call" | custom-call | flops 402653184 | bytes 4194304 | tf_op jit(solution)/shard_map/subtract_last/pallas_call | solution.py:134
Async XLA Ops:
  0.0 32.4 %copy-start = (f32[1024,512]{1,0:T(8,128)S(1)}, f32[1024,512]{1,0:T(8,128)}, u32[]{:S(2)}) copy-start(f32[1024,512]{1,0:T(8,128)} %refs_6_.1) | copy-start | bytes 6291460
  0.0 18.4 %collective-permute-start.5 = (f32[512,512]{1,0:T(8,128)}, f32[512,512]{1,0:T(8,128)S(1)}, u32[]{:S(2)}, u32[]{:S(2)}) collective-permute-start(f32[512,512]{1,0:T(8,128)} %mine_ref.1), channel_id=1, source_target_pairs={{0,1},{1,0},{2,3},{3,2},{4,5},{5,4},{6,7},{7,6},{8,9},{9,8},{10,11... | collective-permute-start | bytes 3145736 | tf_op jit(solution)/shard_map/ppermute | solution.py:148
  1.7 8.2 %collective-permute-start = (f32[64,1024]{1,0:T(8,128)S(1)}, f32[64,1024]{1,0:T(8,128)S(1)}, u32[]{:S(2)}, u32[]{:S(2)}) collective-permute-start(f32[64,1024]{1,0:T(8,128)S(1)} %divide_bitcast_fusion.refs_0_), channel_id=1, source_target_pairs={{0,2},{1,5},{2,0},{3,7},{4,6},{5,1},{6,4},{7,3},{8,10},{9,13},{10,... | collective-permute-start | bytes 786440 | tf_op jit(solution)/shard_map/ppermute | solution.py:31
  4.2 13.8 %collective-permute-start.1 = (f32[64,1024]{1,0:T(8,128)S(1)}, f32[64,1024]{1,0:T(8,128)S(1)}, u32[]{:S(2)}, u32[]{:S(2)}) collective-permute-start(f32[64,1024]{1,0:T(8,128)S(1)} %divide_bitcast_fusion.refs_0_), channel_id=1, source_target_pairs={{0,8},{1,9},{2,10},{3,11},{4,12},{5,13},{6,14},{7,15},{8,0},{9,1},... | collective-permute-start | bytes 786440 | tf_op jit(solution)/shard_map/ppermute | solution.py:31
  5.8 14.9 %collective-permute-start.3 = (f32[64,1024]{1,0:T(8,128)S(1)}, f32[64,1024]{1,0:T(8,128)S(1)}, u32[]{:S(2)}, u32[]{:S(2)}) collective-permute-start(f32[64,1024]{1,0:T(8,128)S(1)} %divide_bitcast_fusion.refs_0_), channel_id=1, source_target_pairs={{0,16},{1,17},{2,18},{3,19},{4,20},{5,21},{6,22},{7,23},{8,24},{9,... | collective-permute-start | bytes 786440 | tf_op jit(solution)/shard_map/ppermute | solution.py:31
  8.4 12.3 %collective-permute-start.4 = (f32[64,1024]{1,0:T(8,128)S(1)}, f32[64,1024]{1,0:T(8,128)S(1)}, u32[]{:S(2)}, u32[]{:S(2)}) collective-permute-start(f32[64,1024]{1,0:T(8,128)S(1)} %divide_bitcast_fusion.refs_0_), channel_id=1, source_target_pairs={{0,4},{1,3},{2,6},{3,1},{4,0},{5,7},{6,2},{7,5},{8,12},{9,11},{10,... | collective-permute-start | bytes 786440 | tf_op jit(solution)/shard_map/ppermute | solution.py:31
  9.9 12.6 %collective-permute-start.2 = (f32[64,1024]{1,0:T(8,128)S(1)}, f32[64,1024]{1,0:T(8,128)S(1)}, u32[]{:S(2)}, u32[]{:S(2)}) collective-permute-start(f32[64,1024]{1,0:T(8,128)S(1)} %collective-permute-done.refs_1_), channel_id=1, source_target_pairs={{0,4},{1,3},{2,6},{3,1},{4,0},{5,7},{6,2},{7,5},{8,12},{9,11},{10,... | collective-permute-start | bytes 786440 | tf_op jit(solution)/shard_map/ppermute | solution.py:31
  18.0 6.4 %collective-permute-start.6 = (f32[64,1024]{1,0:T(8,128)S(1)}, f32[64,1024]{1,0:T(8,128)S(1)}, u32[]{:S(2)}, u32[]{:S(2)}) collective-permute-start(f32[64,1024]{1,0:T(8,128)S(1)} %collective-permute-done.1.refs_2_), channel_id=1, source_target_pairs={{0,2},{1,5},{2,0},{3,7},{4,6},{5,1},{6,4},{7,3},{8,10},{9,13},{10,... | collective-permute-start | bytes 786440 | tf_op jit(solution)/shard_map/ppermute | solution.py:31
  18.4 1.2 %copy-start.1 = (f32[512,512]{1,0:T(8,128)S(1)}, f32[512,512]{1,0:T(8,128)}, u32[]{:S(2)}) copy-start(f32[512,512]{1,0:T(8,128)} %mine_ref.1) | copy-start | bytes 3145732
  20.7 7.2 %collective-permute-start.9 = (f32[64,1024]{1,0:T(8,128)S(1)}, f32[64,1024]{1,0:T(8,128)S(1)}, u32[]{:S(2)}, u32[]{:S(2)}) collective-permute-start(f32[64,1024]{1,0:T(8,128)S(1)} %collective-permute-done.3.refs_0_), channel_id=1, source_target_pairs={{0,8},{1,9},{2,10},{3,11},{4,12},{5,13},{6,14},{7,15},{8,0},{9,1},... | collective-permute-start | bytes 786440 | tf_op jit(solution)/shard_map/ppermute | solution.py:31
  20.8 10.8 %collective-permute-start.13 = (f32[64,1024]{1,0:T(8,128)S(1)}, f32[64,1024]{1,0:T(8,128)S(1)}, u32[]{:S(2)}, u32[]{:S(2)}) collective-permute-start(f32[64,1024]{1,0:T(8,128)S(1)} %collective-permute-done.3.refs_0_), channel_id=1, source_target_pairs={{0,2},{1,5},{2,0},{3,7},{4,6},{5,1},{6,4},{7,3},{8,10},{9,13},{10,... | collective-permute-start | bytes 786440 | tf_op jit(solution)/shard_map/ppermute | solution.py:31
  24.4 9.1 %collective-permute-start.7 = (f32[64,1024]{1,0:T(8,128)S(1)}, f32[64,1024]{1,0:T(8,128)S(1)}, u32[]{:S(2)}, u32[]{:S(2)}) collective-permute-start(f32[64,1024]{1,0:T(8,128)S(1)} %collective-permute-done.3.refs_0_), channel_id=1, source_target_pairs={{0,4},{1,3},{2,6},{3,1},{4,0},{5,7},{6,2},{7,5},{8,12},{9,11},{10,... | collective-permute-start | bytes 786440 | tf_op jit(solution)/shard_map/ppermute | solution.py:31
  27.9 9.1 %collective-permute-start.10 = (f32[64,1024]{1,0:T(8,128)S(1)}, f32[64,1024]{1,0:T(8,128)S(1)}, u32[]{:S(2)}, u32[]{:S(2)}) collective-permute-start(f32[64,1024]{1,0:T(8,128)S(1)} %collective-permute-done.9.refs_3_), channel_id=1, source_target_pairs={{0,2},{1,5},{2,0},{3,7},{4,6},{5,1},{6,4},{7,3},{8,10},{9,13},{10,... | collective-permute-start | bytes 786440 | tf_op jit(solution)/shard_map/ppermute | solution.py:31
  30.0 10.4 %collective-permute-start.12 = (f32[64,1024]{1,0:T(8,128)S(1)}, f32[64,1024]{1,0:T(8,128)S(1)}, u32[]{:S(2)}, u32[]{:S(2)}) collective-permute-start(f32[64,1024]{1,0:T(8,128)S(1)} %collective-permute-done.4.refs_3_), channel_id=1, source_target_pairs={{0,8},{1,9},{2,10},{3,11},{4,12},{5,13},{6,14},{7,15},{8,0},{9,1},... | collective-permute-start | bytes 786440 | tf_op jit(solution)/shard_map/ppermute | solution.py:31
  30.4 10.0 %collective-permute-start.15 = (f32[64,1024]{1,0:T(8,128)S(1)}, f32[64,1024]{1,0:T(8,128)S(1)}, u32[]{:S(2)}, u32[]{:S(2)}) collective-permute-start(f32[64,1024]{1,0:T(8,128)S(1)} %collective-permute-done.6.refs_2_), channel_id=1, source_target_pairs={{0,4},{1,3},{2,6},{3,1},{4,0},{5,7},{6,2},{7,5},{8,12},{9,11},{10,... | collective-permute-start | bytes 786440 | tf_op jit(solution)/shard_map/ppermute | solution.py:31
  31.6 8.8 %collective-permute-start.14 = (f32[64,1024]{1,0:T(8,128)S(1)}, f32[64,1024]{1,0:T(8,128)S(1)}, u32[]{:S(2)}, u32[]{:S(2)}) collective-permute-start(f32[64,1024]{1,0:T(8,128)S(1)} %collective-permute-done.13.refs_4_), channel_id=1, source_target_pairs={{0,4},{1,3},{2,6},{3,1},{4,0},{5,7},{6,2},{7,5},{8,12},{9,11},{10,... | collective-permute-start | bytes 786440 | tf_op jit(solution)/shard_map/ppermute | solution.py:31
  33.5 8.5 %collective-permute-start.8 = (f32[64,1024]{1,0:T(8,128)S(1)}, f32[64,1024]{1,0:T(8,128)S(1)}, u32[]{:S(2)}, u32[]{:S(2)}) collective-permute-start(f32[64,1024]{1,0:T(8,128)S(1)} %collective-permute-done.7.refs_5_), channel_id=1, source_target_pairs={{0,8},{1,9},{2,10},{3,11},{4,12},{5,13},{6,14},{7,15},{8,0},{9,1},... | collective-permute-start | bytes 786440 | tf_op jit(solution)/shard_map/ppermute | solution.py:31
  37.0 6.4 %collective-permute-start.11 = (f32[64,1024]{1,0:T(8,128)S(1)}, f32[64,1024]{1,0:T(8,128)S(1)}, u32[]{:S(2)}, u32[]{:S(2)}) collective-permute-start(f32[64,1024]{1,0:T(8,128)S(1)} %collective-permute-done.10.refs_3_), channel_id=1, source_target_pairs={{0,4},{1,3},{2,6},{3,1},{4,0},{5,7},{6,2},{7,5},{8,12},{9,11},{10,... | collective-permute-start | bytes 786440 | tf_op jit(solution)/shard_map/ppermute | solution.py:31

commit v6 on v4

--- a/solution.py
+++ b/solution.py
@@ -166,7 +166,6 @@
     near_d = send(near_a, second)
     last_a = send(last, first)
     last_b = send(far_b, layer[1])
-    last_a, total = together(last_a, total)
     total = subtract_round(total, (far, own_d, near_a, last), high, low, 1)
     last_d = send(last_a, second)
     total = subtract_round(total, (far_a, far_b, near_b, far_d, near_d, last_a), high, low, 2)

time: 45.2 us -> 45.2 us (level)
  starting transfers between devices: 20 us -> 19.3 us
  waiting for transfers between devices: 16.2 us -> 16.8 us
    ppermute x15, waiting for transfers between devices: 16.2 us -> 16.8 us  [send(): return lax.ppermute(value, ('col', 'row'), pairs)]
    ppermute x15, starting transfers between devices: 19.5 us -> 18.9 us  [send(): return lax.ppermute(value, ('col', 'row'), pairs)]
where the time goes in v6:
time: 45.2 us; the launch traced here: 45 us
  starting transfers between devices  19.3 us (43%)
  waiting for transfers between devices  16.8 us (37%)
  Pallas kernels  6.33 us (14%)
  local copies, waits for them, and re-layouts  1.23 us (3%)
  other arithmetic  1.22 us (3%)
    ppermute x15, starting transfers between devices, send(): return lax.ppermute(value, ('col', 'row'), pairs)  18.9 us
    ppermute x15, waiting for transfers between devices, send(): return lax.ppermute(value, ('col', 'row'), pairs)  16.8 us
    pallas_call x4, Pallas kernels, subtract_round(): pl.pallas_call(functools.partial(last_kernel if last else round_kernel, m...  5.28 us
    unnamed x4, local copies, waits for them, and re-layouts  1.23 us
    div x1, other arithmetic, local_by_layers(): own = phi_slab.T / eigenvalues[:, None]  1.22 us
    pallas_call x1, Pallas kernels, prepare(): pl.pallas_call(functools.partial(prepare_kernel, order), out_shape=(shape...  1.05 us
  transfers between devices with their start and end apart: 16, of which 6 were waited for; matrix products, arithmetic and copies ran while one was open for 3% of the time, Pallas kernels for 10%

profile of v6, /device:TPU:0, one launch (start us, length us, event | category | flops | bytes accessed | tf_op | source)
XLA Modules:
  0.0 45.0 jit_solution(5368731269944886590)
XLA Ops:
  0.0 0.0 copy-start
  0.0 0.5 %collective-permute-start.5 = (f32[512,512]{1,0:T(8,128)}, f32[512,512]{1,0:T(8,128)S(1)}, u32[]{:S(2)}, u32[]{:S(2)}) collective-permute-start(f32[512,512]{1,0:T(8,128)} %mine_ref.1), channel_id=1, source_target_pairs={{0,1},{1,0},{2,3},{3,2},{4,5},{5,4},{6,7},{7,6},{8,9},{9,8},{10,11... | collective-permute-start | bytes 3145736 | tf_op jit(solution)/shard_map/ppermute | solution.py:148
  0.5 1.2 %divide_bitcast_fusion.refs_0_ = f32[64,1024]{1,0:T(8,128)S(1)} fusion(f32[1024,64]{0,1:T(8,128)} %param.5, f32[64]{0:T(128)} %param.7), kind=kLoop, calls=%fused_computation | loop fusion | flops 65536 | bytes 524544 | tf_op jit(solution)/shard_map/div | solution.py:149
  1.7 2.5 %collective-permute-start = (f32[64,1024]{1,0:T(8,128)S(1)}, f32[64,1024]{1,0:T(8,128)S(1)}, u32[]{:S(2)}, u32[]{:S(2)}) collective-permute-start(f32[64,1024]{1,0:T(8,128)S(1)} %divide_bitcast_fusion.refs_0_), channel_id=1, source_target_pairs={{0,2},{1,5},{2,0},{3,7},{4,6},{5,1},{6,4},{7,3},{8,10},{9,13},{10,... | collective-permute-start | bytes 786440 | tf_op jit(solution)/shard_map/ppermute | solution.py:31
  4.2 1.6 %collective-permute-start.1 = (f32[64,1024]{1,0:T(8,128)S(1)}, f32[64,1024]{1,0:T(8,128)S(1)}, u32[]{:S(2)}, u32[]{:S(2)}) collective-permute-start(f32[64,1024]{1,0:T(8,128)S(1)} %divide_bitcast_fusion.refs_0_), channel_id=1, source_target_pairs={{0,8},{1,9},{2,10},{3,11},{4,12},{5,13},{6,14},{7,15},{8,0},{9,1},... | collective-permute-start | bytes 786440 | tf_op jit(solution)/shard_map/ppermute | solution.py:31
  5.8 2.6 %collective-permute-start.3 = (f32[64,1024]{1,0:T(8,128)S(1)}, f32[64,1024]{1,0:T(8,128)S(1)}, u32[]{:S(2)}, u32[]{:S(2)}) collective-permute-start(f32[64,1024]{1,0:T(8,128)S(1)} %divide_bitcast_fusion.refs_0_), channel_id=1, source_target_pairs={{0,16},{1,17},{2,18},{3,19},{4,20},{5,21},{6,22},{7,23},{8,24},{9,... | collective-permute-start | bytes 786440 | tf_op jit(solution)/shard_map/ppermute | solution.py:31
  8.4 1.5 %collective-permute-start.4 = (f32[64,1024]{1,0:T(8,128)S(1)}, f32[64,1024]{1,0:T(8,128)S(1)}, u32[]{:S(2)}, u32[]{:S(2)}) collective-permute-start(f32[64,1024]{1,0:T(8,128)S(1)} %divide_bitcast_fusion.refs_0_), channel_id=1, source_target_pairs={{0,4},{1,3},{2,6},{3,1},{4,0},{5,7},{6,2},{7,5},{8,12},{9,11},{10,... | collective-permute-start | bytes 786440 | tf_op jit(solution)/shard_map/ppermute | solution.py:31
  9.9 0.0 collective-permute-done.refs_1_
  9.9 0.7 %collective-permute-start.2 = (f32[64,1024]{1,0:T(8,128)S(1)}, f32[64,1024]{1,0:T(8,128)S(1)}, u32[]{:S(2)}, u32[]{:S(2)}) collective-permute-start(f32[64,1024]{1,0:T(8,128)S(1)} %collective-permute-done.refs_1_), channel_id=1, source_target_pairs={{0,4},{1,3},{2,6},{3,1},{4,0},{5,7},{6,2},{7,5},{8,12},{9,11},{10,... | collective-permute-start | bytes 786440 | tf_op jit(solution)/shard_map/ppermute | solution.py:31
  10.6 7.4 %collective-permute-done.1.refs_2_ = f32[64,1024]{1,0:T(8,128)S(1)} collective-permute-done((f32[64,1024]{1,0:T(8,128)S(1)}, f32[64,1024]{1,0:T(8,128)S(1)}, u32[]{:S(2)}, u32[]{:S(2)}) %collective-permute-start.1) | collective-permute-done | bytes 262176 | tf_op jit(solution)/shard_map/ppermute | solution.py:31
  18.0 0.4 collective-permute-start.6
  18.4 0.0 collective-permute-done.5.other_ref
  18.4 0.0 copy-start.1
  18.4 1.2 %copy-done.1 = f32[512,512]{1,0:T(8,128)S(1)} copy-done((f32[512,512]{1,0:T(8,128)S(1)}, f32[512,512]{1,0:T(8,128)}, u32[]{:S(2)}) %copy-start.1) | copy-done | bytes 1048600
  19.6 1.1 %prepare_cols.1 = (bf16[1024,512]{1,0:T(8,128)(2,1)S(1)}, bf16[1024,512]{1,0:T(8,128)(2,1)S(1)}) custom-call(f32[512,512]{1,0:T(8,128)S(1)} %copy-done.1, f32[512,512]{1,0:T(8,128)S(1)} %collective-permute-done.5.other_ref), custom_call_target="tpu_custom_call" | custom-call | bytes 4194304 | tf_op jit(solution)/shard_map/prepare_cols/pallas_call | solution.py:81
  20.7 0.0 collective-permute-done.3.refs_0_
  20.7 0.0 collective-permute-done.4.refs_3_
  20.7 0.1 collective-permute-start.9
  20.8 1.7 %collective-permute-start.12 = (f32[64,1024]{1,0:T(8,128)S(1)}, f32[64,1024]{1,0:T(8,128)S(1)}, u32[]{:S(2)}, u32[]{:S(2)}) collective-permute-start(f32[64,1024]{1,0:T(8,128)S(1)} %collective-permute-done.3.refs_0_), channel_id=1, source_target_pairs={{0,2},{1,5},{2,0},{3,7},{4,6},{5,1},{6,4},{7,3},{8,10},{9,13},{10,... | collective-permute-start | bytes 786440 | tf_op jit(solution)/shard_map/ppermute | solution.py:31
  22.5 0.0 collective-permute-done.2.refs_1_
  22.5 1.9 %collective-permute-done.6.refs_2_ = f32[64,1024]{1,0:T(8,128)S(1)} collective-permute-done((f32[64,1024]{1,0:T(8,128)S(1)}, f32[64,1024]{1,0:T(8,128)S(1)}, u32[]{:S(2)}, u32[]{:S(2)}) %collective-permute-start.6) | collective-permute-done | bytes 262176 | tf_op jit(solution)/shard_map/ppermute | solution.py:31
  24.4 0.4 collective-permute-start.7
  24.8 3.1 %collective-permute-done.9.refs_3_ = f32[64,1024]{1,0:T(8,128)S(1)} collective-permute-done((f32[64,1024]{1,0:T(8,128)S(1)}, f32[64,1024]{1,0:T(8,128)S(1)}, u32[]{:S(2)}, u32[]{:S(2)}) %collective-permute-start.9) | collective-permute-done | bytes 262176 | tf_op jit(solution)/shard_map/ppermute | solution.py:31
  27.9 2.1 %collective-permute-start.10 = (f32[64,1024]{1,0:T(8,128)S(1)}, f32[64,1024]{1,0:T(8,128)S(1)}, u32[]{:S(2)}, u32[]{:S(2)}) collective-permute-start(f32[64,1024]{1,0:T(8,128)S(1)} %collective-permute-done.9.refs_3_), channel_id=1, source_target_pairs={{0,2},{1,5},{2,0},{3,7},{4,6},{5,1},{6,4},{7,3},{8,10},{9,13},{10,... | collective-permute-start | bytes 786440 | tf_op jit(solution)/shard_map/ppermute | solution.py:31
  30.0 0.4 collective-permute-start.13
  30.4 1.2 %collective-permute-start.15 = (f32[64,1024]{1,0:T(8,128)S(1)}, f32[64,1024]{1,0:T(8,128)S(1)}, u32[]{:S(2)}, u32[]{:S(2)}) collective-permute-start(f32[64,1024]{1,0:T(8,128)S(1)} %collective-permute-done.6.refs_2_), channel_id=1, source_target_pairs={{0,4},{1,3},{2,6},{3,1},{4,0},{5,7},{6,2},{7,5},{8,12},{9,11},{10,... | collective-permute-start | bytes 786440 | tf_op jit(solution)/shard_map/ppermute | solution.py:31
  31.6 0.0 collective-permute-done.12.refs_0_
  31.6 0.8 %collective-permute-start.14 = (f32[64,1024]{1,0:T(8,128)S(1)}, f32[64,1024]{1,0:T(8,128)S(1)}, u32[]{:S(2)}, u32[]{:S(2)}) collective-permute-start(f32[64,1024]{1,0:T(8,128)S(1)} %collective-permute-done.12.refs_0_), channel_id=1, source_target_pairs={{0,4},{1,3},{2,6},{3,1},{4,0},{5,7},{6,2},{7,5},{8,12},{9,11},{10,... | collective-permute-start | bytes 786440 | tf_op jit(solution)/shard_map/ppermute | solution.py:31
  32.4 0.6 %collective-permute-done.7.refs_1_ = f32[64,1024]{1,0:T(8,128)S(1)} collective-permute-done((f32[64,1024]{1,0:T(8,128)S(1)}, f32[64,1024]{1,0:T(8,128)S(1)}, u32[]{:S(2)}, u32[]{:S(2)}) %collective-permute-start.7) | collective-permute-done | bytes 262176 | tf_op jit(solution)/shard_map/ppermute | solution.py:31
  33.0 1.0 %collective-permute-start.8 = (f32[64,1024]{1,0:T(8,128)S(1)}, f32[64,1024]{1,0:T(8,128)S(1)}, u32[]{:S(2)}, u32[]{:S(2)}) collective-permute-start(f32[64,1024]{1,0:T(8,128)S(1)} %collective-permute-done.7.refs_1_), channel_id=1, source_target_pairs={{0,8},{1,9},{2,10},{3,11},{4,12},{5,13},{6,14},{7,15},{8,0},{9,1},... | collective-permute-start | bytes 786440 | tf_op jit(solution)/shard_map/ppermute | solution.py:31
  34.1 2.9 %collective-permute-done.10.refs_5_ = f32[64,1024]{1,0:T(8,128)S(1)} collective-permute-done((f32[64,1024]{1,0:T(8,128)S(1)}, f32[64,1024]{1,0:T(8,128)S(1)}, u32[]{:S(2)}, u32[]{:S(2)}) %collective-permute-start.10) | collective-permute-done | bytes 262176 | tf_op jit(solution)/shard_map/ppermute | solution.py:31
  37.0 1.8 %collective-permute-start.11 = (f32[64,1024]{1,0:T(8,128)S(1)}, f32[64,1024]{1,0:T(8,128)S(1)}, u32[]{:S(2)}, u32[]{:S(2)}) collective-permute-start(f32[64,1024]{1,0:T(8,128)S(1)} %collective-permute-done.10.refs_5_), channel_id=1, source_target_pairs={{0,4},{1,3},{2,6},{3,1},{4,0},{5,7},{6,2},{7,5},{8,12},{9,11},{10,... | collective-permute-start | bytes 786440 | tf_op jit(solution)/shard_map/ppermute | solution.py:31
  38.8 0.0 copy-done
  38.8 1.0 %subtract_round.3.refs_6_ = f32[1024,512]{1,0:T(8,128)S(1)} custom-call(f32[64,1024]{1,0:T(8,128)S(1)} %divide_bitcast_fusion.refs_0_, f32[64,1024]{1,0:T(8,128)S(1)} %collective-permute-done.refs_1_, f32[64,1024]{1,0:T(8,128)S(1)} %collective-permute-done.1.refs_2_, f32[64,1024]{1,0:T(8,128)S(1)} %collective-permute-done.4.refs_3_, ...), custom_call_target="tpu_custom_call" | custom-call | flops 805306368 | bytes 4194304 | tf_op jit(solution)/shard_map/subtract_round/pallas_call | solution.py:134
  39.9 1.0 %subtract_round.4.refs_8_ = f32[1024,512]{1,0:T(8,128)S(1)} custom-call(f32[64,1024]{1,0:T(8,128)S(1)} %collective-permute-done.3.refs_0_, f32[64,1024]{1,0:T(8,128)S(1)} %collective-permute-done.2.refs_1_, f32[64,1024]{1,0:T(8,128)S(1)} %collective-permute-done.6.refs_2_, f32[64,1024]{1,0:T(8,128)S(1)} %collective-permute-done.9.refs_3_, ...), custom_call_target="tpu_custom_call" | custom-call | flops 805306368 | bytes 4194304 | tf_op jit(solution)/shard_map/subtract_round/pallas_call | solution.py:134
  40.9 0.0 collective-permute-done.13.refs_2_
  40.9 0.0 collective-permute-done.15.refs_4_
  40.9 0.0 collective-permute-done.14.refs_3_
  40.9 1.6 %subtract_round.5.refs_4_ = f32[1024,512]{1,0:T(8,128)S(1)} custom-call(f32[64,1024]{1,0:T(8,128)S(1)} %collective-permute-done.12.refs_0_, f32[64,1024]{1,0:T(8,128)S(1)} %collective-permute-done.7.refs_1_, f32[64,1024]{1,0:T(8,128)S(1)} %collective-permute-done.13.refs_2_, f32[64,1024]{1,0:T(8,128)S(1)} %collective-permute-done.14.refs_3_, ...), custom_call_target="tpu_custom_call" | custom-call | flops 1207959552 | bytes 4194304 | tf_op jit(solution)/shard_map/subtract_round/pallas_call | solution.py:134
  42.5 0.0 collective-permute-done.8.refs_0_
  42.5 0.9 %collective-permute-done.11.refs_1_ = f32[64,1024]{1,0:T(8,128)S(1)} collective-permute-done((f32[64,1024]{1,0:T(8,128)S(1)}, f32[64,1024]{1,0:T(8,128)S(1)}, u32[]{:S(2)}, u32[]{:S(2)}) %collective-permute-start.11) | collective-permute-done | bytes 262176 | tf_op jit(solution)/shard_map/ppermute | solution.py:31
  43.4 1.6 %subtract_last.1 = f32[1024,512]{1,0:T(8,128)} custom-call(f32[64,1024]{1,0:T(8,128)S(1)} %collective-permute-done.8.refs_0_, f32[64,1024]{1,0:T(8,128)S(1)} %collective-permute-done.11.refs_1_, bf16[1024,512]{1,0:T(8,128)(2,1)S(1)} %get-tuple-element.24.refs_4_.refs_6_.refs_2_, bf16[1024,512]{1,0:T(8,128)(2,1)S(1)} %get-tuple-element.25.refs_5_.refs_7_.refs_3_, ...), custom_call_target="tpu_custom_call" | custom-call | flops 402653184 | bytes 4194304 | tf_op jit(solution)/shard_map/subtract_last/pallas_call | solution.py:134
Async XLA Ops:
  0.0 38.8 %copy-start = (f32[1024,512]{1,0:T(8,128)S(1)}, f32[1024,512]{1,0:T(8,128)}, u32[]{:S(2)}) copy-start(f32[1024,512]{1,0:T(8,128)} %refs_6_.1) | copy-start | bytes 6291460
  0.0 18.4 %collective-permute-start.5 = (f32[512,512]{1,0:T(8,128)}, f32[512,512]{1,0:T(8,128)S(1)}, u32[]{:S(2)}, u32[]{:S(2)}) collective-permute-start(f32[512,512]{1,0:T(8,128)} %mine_ref.1), channel_id=1, source_target_pairs={{0,1},{1,0},{2,3},{3,2},{4,5},{5,4},{6,7},{7,6},{8,9},{9,8},{10,11... | collective-permute-start | bytes 3145736 | tf_op jit(solution)/shard_map/ppermute | solution.py:148
  1.7 8.2 %collective-permute-start = (f32[64,1024]{1,0:T(8,128)S(1)}, f32[64,1024]{1,0:T(8,128)S(1)}, u32[]{:S(2)}, u32[]{:S(2)}) collective-permute-start(f32[64,1024]{1,0:T(8,128)S(1)} %divide_bitcast_fusion.refs_0_), channel_id=1, source_target_pairs={{0,2},{1,5},{2,0},{3,7},{4,6},{5,1},{6,4},{7,3},{8,10},{9,13},{10,... | collective-permute-start | bytes 786440 | tf_op jit(solution)/shard_map/ppermute | solution.py:31
  4.2 13.8 %collective-permute-start.1 = (f32[64,1024]{1,0:T(8,128)S(1)}, f32[64,1024]{1,0:T(8,128)S(1)}, u32[]{:S(2)}, u32[]{:S(2)}) collective-permute-start(f32[64,1024]{1,0:T(8,128)S(1)} %divide_bitcast_fusion.refs_0_), channel_id=1, source_target_pairs={{0,8},{1,9},{2,10},{3,11},{4,12},{5,13},{6,14},{7,15},{8,0},{9,1},... | collective-permute-start | bytes 786440 | tf_op jit(solution)/shard_map/ppermute | solution.py:31
  5.8 14.9 %collective-permute-start.3 = (f32[64,1024]{1,0:T(8,128)S(1)}, f32[64,1024]{1,0:T(8,128)S(1)}, u32[]{:S(2)}, u32[]{:S(2)}) collective-permute-start(f32[64,1024]{1,0:T(8,128)S(1)} %divide_bitcast_fusion.refs_0_), channel_id=1, source_target_pairs={{0,16},{1,17},{2,18},{3,19},{4,20},{5,21},{6,22},{7,23},{8,24},{9,... | collective-permute-start | bytes 786440 | tf_op jit(solution)/shard_map/ppermute | solution.py:31
  8.4 12.3 %collective-permute-start.4 = (f32[64,1024]{1,0:T(8,128)S(1)}, f32[64,1024]{1,0:T(8,128)S(1)}, u32[]{:S(2)}, u32[]{:S(2)}) collective-permute-start(f32[64,1024]{1,0:T(8,128)S(1)} %divide_bitcast_fusion.refs_0_), channel_id=1, source_target_pairs={{0,4},{1,3},{2,6},{3,1},{4,0},{5,7},{6,2},{7,5},{8,12},{9,11},{10,... | collective-permute-start | bytes 786440 | tf_op jit(solution)/shard_map/ppermute | solution.py:31
  9.9 12.6 %collective-permute-start.2 = (f32[64,1024]{1,0:T(8,128)S(1)}, f32[64,1024]{1,0:T(8,128)S(1)}, u32[]{:S(2)}, u32[]{:S(2)}) collective-permute-start(f32[64,1024]{1,0:T(8,128)S(1)} %collective-permute-done.refs_1_), channel_id=1, source_target_pairs={{0,4},{1,3},{2,6},{3,1},{4,0},{5,7},{6,2},{7,5},{8,12},{9,11},{10,... | collective-permute-start | bytes 786440 | tf_op jit(solution)/shard_map/ppermute | solution.py:31
  18.0 6.4 %collective-permute-start.6 = (f32[64,1024]{1,0:T(8,128)S(1)}, f32[64,1024]{1,0:T(8,128)S(1)}, u32[]{:S(2)}, u32[]{:S(2)}) collective-permute-start(f32[64,1024]{1,0:T(8,128)S(1)} %collective-permute-done.1.refs_2_), channel_id=1, source_target_pairs={{0,2},{1,5},{2,0},{3,7},{4,6},{5,1},{6,4},{7,3},{8,10},{9,13},{10,... | collective-permute-start | bytes 786440 | tf_op jit(solution)/shard_map/ppermute | solution.py:31
  18.4 1.2 %copy-start.1 = (f32[512,512]{1,0:T(8,128)S(1)}, f32[512,512]{1,0:T(8,128)}, u32[]{:S(2)}) copy-start(f32[512,512]{1,0:T(8,128)} %mine_ref.1) | copy-start | bytes 3145732
  20.7 7.2 %collective-permute-start.9 = (f32[64,1024]{1,0:T(8,128)S(1)}, f32[64,1024]{1,0:T(8,128)S(1)}, u32[]{:S(2)}, u32[]{:S(2)}) collective-permute-start(f32[64,1024]{1,0:T(8,128)S(1)} %collective-permute-done.3.refs_0_), channel_id=1, source_target_pairs={{0,8},{1,9},{2,10},{3,11},{4,12},{5,13},{6,14},{7,15},{8,0},{9,1},... | collective-permute-start | bytes 786440 | tf_op jit(solution)/shard_map/ppermute | solution.py:31
  20.8 10.8 %collective-permute-start.12 = (f32[64,1024]{1,0:T(8,128)S(1)}, f32[64,1024]{1,0:T(8,128)S(1)}, u32[]{:S(2)}, u32[]{:S(2)}) collective-permute-start(f32[64,1024]{1,0:T(8,128)S(1)} %collective-permute-done.3.refs_0_), channel_id=1, source_target_pairs={{0,2},{1,5},{2,0},{3,7},{4,6},{5,1},{6,4},{7,3},{8,10},{9,13},{10,... | collective-permute-start | bytes 786440 | tf_op jit(solution)/shard_map/ppermute | solution.py:31
  24.4 8.6 %collective-permute-start.7 = (f32[64,1024]{1,0:T(8,128)S(1)}, f32[64,1024]{1,0:T(8,128)S(1)}, u32[]{:S(2)}, u32[]{:S(2)}) collective-permute-start(f32[64,1024]{1,0:T(8,128)S(1)} %collective-permute-done.3.refs_0_), channel_id=1, source_target_pairs={{0,4},{1,3},{2,6},{3,1},{4,0},{5,7},{6,2},{7,5},{8,12},{9,11},{10,... | collective-permute-start | bytes 786440 | tf_op jit(solution)/shard_map/ppermute | solution.py:31
  27.9 9.1 %collective-permute-start.10 = (f32[64,1024]{1,0:T(8,128)S(1)}, f32[64,1024]{1,0:T(8,128)S(1)}, u32[]{:S(2)}, u32[]{:S(2)}) collective-permute-start(f32[64,1024]{1,0:T(8,128)S(1)} %collective-permute-done.9.refs_3_), channel_id=1, source_target_pairs={{0,2},{1,5},{2,0},{3,7},{4,6},{5,1},{6,4},{7,3},{8,10},{9,13},{10,... | collective-permute-start | bytes 786440 | tf_op jit(solution)/shard_map/ppermute | solution.py:31
  30.0 10.9 %collective-permute-start.13 = (f32[64,1024]{1,0:T(8,128)S(1)}, f32[64,1024]{1,0:T(8,128)S(1)}, u32[]{:S(2)}, u32[]{:S(2)}) collective-permute-start(f32[64,1024]{1,0:T(8,128)S(1)} %collective-permute-done.4.refs_3_), channel_id=1, source_target_pairs={{0,8},{1,9},{2,10},{3,11},{4,12},{5,13},{6,14},{7,15},{8,0},{9,1},... | collective-permute-start | bytes 786440 | tf_op jit(solution)/shard_map/ppermute | solution.py:31
  30.4 10.5 %collective-permute-start.15 = (f32[64,1024]{1,0:T(8,128)S(1)}, f32[64,1024]{1,0:T(8,128)S(1)}, u32[]{:S(2)}, u32[]{:S(2)}) collective-permute-start(f32[64,1024]{1,0:T(8,128)S(1)} %collective-permute-done.6.refs_2_), channel_id=1, source_target_pairs={{0,4},{1,3},{2,6},{3,1},{4,0},{5,7},{6,2},{7,5},{8,12},{9,11},{10,... | collective-permute-start | bytes 786440 | tf_op jit(solution)/shard_map/ppermute | solution.py:31
  31.6 9.3 %collective-permute-start.14 = (f32[64,1024]{1,0:T(8,128)S(1)}, f32[64,1024]{1,0:T(8,128)S(1)}, u32[]{:S(2)}, u32[]{:S(2)}) collective-permute-start(f32[64,1024]{1,0:T(8,128)S(1)} %collective-permute-done.12.refs_0_), channel_id=1, source_target_pairs={{0,4},{1,3},{2,6},{3,1},{4,0},{5,7},{6,2},{7,5},{8,12},{9,11},{10,... | collective-permute-start | bytes 786440 | tf_op jit(solution)/shard_map/ppermute | solution.py:31
  33.0 9.5 %collective-permute-start.8 = (f32[64,1024]{1,0:T(8,128)S(1)}, f32[64,1024]{1,0:T(8,128)S(1)}, u32[]{:S(2)}, u32[]{:S(2)}) collective-permute-start(f32[64,1024]{1,0:T(8,128)S(1)} %collective-permute-done.7.refs_1_), channel_id=1, source_target_pairs={{0,8},{1,9},{2,10},{3,11},{4,12},{5,13},{6,14},{7,15},{8,0},{9,1},... | collective-permute-start | bytes 786440 | tf_op jit(solution)/shard_map/ppermute | solution.py:31
  37.0 6.4 %collective-permute-start.11 = (f32[64,1024]{1,0:T(8,128)S(1)}, f32[64,1024]{1,0:T(8,128)S(1)}, u32[]{:S(2)}, u32[]{:S(2)}) collective-permute-start(f32[64,1024]{1,0:T(8,128)S(1)} %collective-permute-done.10.refs_5_), channel_id=1, source_target_pairs={{0,4},{1,3},{2,6},{3,1},{4,0},{5,7},{6,2},{7,5},{8,12},{9,11},{10,... | collective-permute-start | bytes 786440 | tf_op jit(solution)/shard_map/ppermute | solution.py:31
